TPU v7x, 512 devices: a whole 4x4x16 slice. The times are simulated.
512 devices in a mesh: rep: 64 (over y, z_lo, x), fsdp: 8 (over z_hi, core).
Axes of the slice: x: 4, y: 4, z: 16 (z_hi: 4, z_lo: 4; z = z_hi * 4 + z_lo), core: 2. Of those that a mesh axis runs over, the one named last changes fastest.
Arguments:
- activations: bfloat16 [64, 1536, 5120], P('rep', 'fsdp'), may hold values from -6 to 6
- doc_ids: int32 [64, 1536], P('rep', 'fsdp'), may hold values from 0 to 15, never falling along the last dimension, each value on 1 to 192 neighbouring positions
- step_index: int32 [1], replicated, may hold values from 0 to 63
- proj_weights: bfloat16 [64, 5120, 384], P('rep', 'fsdp'), may hold values from -1 to 1
- first_moment: bfloat16 [64, 5120, 384], P('rep', 'fsdp'), may hold values from -12 to 12
- second_moment: bfloat16 [64, 5120, 384], P('rep', 'fsdp'), may hold values from 0.0099487305 to 100
- out_grad: bfloat16 [64, 1536, 128], P('rep', 'fsdp'), may hold values from -6 to 6
Outputs:
- mixed_weights: bfloat16 [64, 5120, 384], P('rep', 'fsdp')
- first_next: bfloat16 [64, 5120, 384], P('rep', 'fsdp')
- second_next: bfloat16 [64, 5120, 384], P('rep', 'fsdp')
All inputs are finite; a program needn't handle non-finite values.
Results may differ from a plain program's by a relative error of at most 0.035.
Values may be sent and summed in bfloat16 or wider, within the bound.
A program may use at most 64 MiB of HBM per device.

v0:
```python
import jax
import jax.numpy as jnp
from jax import lax
from jax.sharding import PartitionSpec as P

BETA_ONE = 0.9
BETA_TWO = 0.95
LEARN_RATE = 0.002
DECAY_RATE = 0.1
ADAM_EPS = 1e-08


def as_sent(value):
    return jax.tree.map(lambda a: a.astype(jnp.bfloat16) if a.dtype == jnp.float32 else a, value)


def partner(value, axis, distance):
    return lax.ppermute(value, axis, [(i, i ^ 1 << distance) for i in range(lax.axis_size(axis))])


def rms_rows(activ_rows):
    values = activ_rows.astype(jnp.float32)
    scale = lax.rsqrt(jnp.mean(values * values, axis=-1, keepdims=True) + 1e-05)
    return (values * scale).astype(jnp.bfloat16)


def rotate(block, cosine_tab, sine_tab):
    half = block.shape[1] // 2
    first = block[:, :half]
    second = block[:, half:]
    return jnp.concatenate(
        [first * cosine_tab - second * sine_tab, first * sine_tab + second * cosine_tab], axis=1
    )


def attend(projected, doc_row):
    length = projected.shape[0]
    head_dim = projected.shape[1] // 3
    query = projected[:, :head_dim]
    keys = projected[:, head_dim : 2 * head_dim]
    values = projected[:, 2 * head_dim :]
    position = jnp.arange(length).astype(jnp.float32)
    inverse = 10000.0 ** (-(jnp.arange(head_dim // 2).astype(jnp.float32) * 2.0 / head_dim))
    angles = position[:, None] * inverse[None, :]
    cosine_tab = jnp.cos(angles)
    sine_tab = jnp.sin(angles)
    query = rotate(query, cosine_tab, sine_tab)
    keys = rotate(keys, cosine_tab, sine_tab)
    scores = jnp.dot(query, keys.T, precision=lax.Precision.HIGHEST) * head_dim ** (-0.5)
    places = jnp.arange(length)
    allowed = (places[None, :] <= places[:, None]) & (doc_row[:, None] == doc_row[None, :])
    scores = jnp.where(allowed, scores, -1e30)
    row_max = lax.stop_gradient(jnp.max(scores, axis=1, keepdims=True))
    expo = jnp.exp(scores - row_max)
    probs = (expo / jnp.sum(expo, axis=1, keepdims=True)).astype(jnp.bfloat16)
    return jnp.dot(probs, values.astype(jnp.bfloat16), preferred_element_type=jnp.float32)


def adam_update(shard, grad, first, second, step_index):
    count = (step_index[0] + 1).astype(jnp.float32)
    weights = shard.astype(jnp.float32)
    first_new = BETA_ONE * first.astype(jnp.float32) + (1.0 - BETA_ONE) * grad
    second_new = BETA_TWO * second.astype(jnp.float32) + (1.0 - BETA_TWO) * grad * grad
    first_hat = first_new / (1.0 - jnp.power(BETA_ONE, count))
    second_hat = second_new / (1.0 - jnp.power(BETA_TWO, count))
    updated = weights - LEARN_RATE * (
        first_hat / (jnp.sqrt(second_hat) + ADAM_EPS) + DECAY_RATE * weights
    )
    return (
        updated.astype(jnp.bfloat16),
        first_new.astype(jnp.bfloat16),
        second_new.astype(jnp.bfloat16),
    )


def swap_with(shard, bit_number):
    return jax.tree.map(
        lambda part, own: part.astype(own.dtype), partner(as_sent(shard), "rep", bit_number), shard
    )


def per_device(
    activations, doc_ids, step_index, proj_weights, first_moment, second_moment, out_grad
):
    activ_rows = activations[0]
    doc_row = doc_ids[0]
    local_rows = proj_weights[0]
    normed = rms_rows(activ_rows)
    features = normed
    projected = jnp.dot(
        features,
        lax.all_gather(local_rows, "fsdp", axis=0, tiled=True),
        preferred_element_type=jnp.float32,
    ).astype(jnp.bfloat16)
    result, pullback = jax.vjp(lambda inner: attend(inner, doc_row), projected.astype(jnp.float32))
    proj_grad = pullback(out_grad[0].astype(jnp.float32))[0].astype(jnp.bfloat16)
    features = normed
    grad = lax.psum_scatter(
        lax.dot_general(
            features, proj_grad, (((0,), (0,)), ((), ())), preferred_element_type=jnp.float32
        ).astype(jnp.bfloat16),
        "fsdp",
        scatter_dimension=0,
        tiled=True,
    ).astype(jnp.float32)
    updated, first_next, second_next = adam_update(
        local_rows, grad, first_moment[0], second_moment[0], step_index
    )
    bit_total = lax.axis_size("rep").bit_length() - 1
    level = step_index[0] % bit_total
    branches = [partial_swap(bit_number) for bit_number in range(bit_total)]
    partner_rows = lax.switch(level, branches, updated)
    mixed_weights = ((updated.astype(jnp.float32) + partner_rows.astype(jnp.float32)) * 0.5).astype(
        jnp.bfloat16
    )
    return (mixed_weights[None], first_next[None], second_next[None])


def partial_swap(bit_number):

    def runner(shard):
        return swap_with(shard, bit_number)

    return runner


def solution(mesh):
    placed = (
        P("rep", "fsdp", None),
        P("rep", "fsdp"),
        P(),
        P("rep", "fsdp", None),
        P("rep", "fsdp", None),
        P("rep", "fsdp", None),
        P("rep", "fsdp", None),
    )
    return jax.shard_map(
        per_device,
        mesh=mesh,
        in_specs=placed,
        out_specs=(P("rep", "fsdp", None), P("rep", "fsdp", None), P("rep", "fsdp", None)),
        check_vma=False,
    )
```

profile of v0, /device:TPU:1, one launch (start us, length us, event | category | flops | bytes accessed | tf_op | source)
XLA Modules:
  0.0 252.8 jit_solution(5568363959128857357)
XLA Ops:
  7.2 0.0 copy-start
  7.2 0.0 all-gather.3.cloned.1.call-start
  7.2 0.7 all-gather.3.cloned.1.call-update
  7.9 0.0 reduce-scatter.2.cloned.1.call-start
  8.0 2.0 fusion
  10.0 0.0 copy-start.5
  10.0 98.5 %all-gather.3.cloned.1.call-done = bf16[1,5120,384]{2,1,0:T(8,128)(2,1)} async-done(((bf16[1,640,384]{2,1,0:T(8,128)(2,1)}), bf16[1,5120,384]{2,1,0:T(8,128)(2,1)}) %all-gather.3.cloned.1.call-update) | async-done | bytes 3932176 | tf_op jit(solution)/shard_map/all_gather | solution.py:92
  108.5 4.0 %fusion.63 = (f32[192,384]{1,0:T(8,128)S(1)}, bf16[192,384]{1,0:T(8,128)(2,1)S(1)}) fusion(bf16[1,5120,384]{2,1,0:T(8,128)(2,1)} %all-gather.3.cloned.1.call-done, bf16[1,192,5120]{2,1,0:T(8,128)(2,1)} %param.13, f32[192]{0:T(256)S(1)} %add_rsqrt_fusion), kind=kOutput, calls=%fused_computation.84 | convolution fusion | flops 758071296 | bytes 6341376 | tf_op jit(solution)/shard_map/dot_general | solution.py:90
  112.5 0.0 copy-start.2
  112.5 0.5 fusion.43
  113.0 0.0 copy-done.5
  113.0 0.4 fusion.64
  113.4 0.1 fusion.42
  113.5 0.0 copy-done
  113.5 0.2 convolution_convert_fusion.2
  113.7 0.2 fusion.23
  113.9 0.5 fusion.54
  114.5 0.4 fusion.55
  114.9 0.5 fusion.47
  115.3 0.1 pad_add_fusion
  115.5 0.0 copy-done.2
  115.5 3.6 %convolution_convert_fusion = bf16[5120,384]{1,0:T(8,128)(2,1)} fusion(bf16[1,192,5120]{2,1,0:T(8,128)(2,1)S(1)} %copy-done.2, f32[192]{0:T(256)S(1)} %add_rsqrt_fusion, f32[192,128]{1,0:T(8,128)S(1)} %get-tuple-element.41, f32[192,128]{1,0:T(8,128)S(1)} %get-tuple-element.42, bf16[192,128]{1,0:T(8,128)(2,1)S(1)} %convolution_convert_fusion.2), kind=kOutput, calls=%fused_computation | convolution fusion | flops 760184832 | bytes 6144768 | tf_op jit(solution)/shard_map/dot_general | solution.py:99
  119.0 0.0 copy-start.1
  119.1 0.0 copy-start.3
  119.1 0.0 copy-start.4
  119.1 0.0 reduce-scatter.2.cloned.1.call-update
  119.9 96.3 %reduce-scatter.2.cloned.1.call-done = bf16[640,384]{1,0:T(8,128)(2,1)} async-done(((bf16[5120,384]{1,0:T(8,128)(2,1)}), bf16[640,384]{1,0:T(8,128)(2,1)}) %reduce-scatter.2.cloned.1.call-update) | async-done | bytes 491536 | tf_op jit(solution)/shard_map/reduce_scatter | solution.py:98
  216.3 0.0 copy-done.1
  216.3 0.0 copy-done.3
  216.3 0.0 copy-done.4
  216.3 2.9 %fusion.18 = (bf16[1,640,384]{2,1,0:T(8,128)(2,1)}, bf16[640,384]{1,0:T(8,128)(2,1)S(1)}, bf16[1,640,384]{2,1,0:T(8,128)(2,1)}) fusion(bf16[640,384]{1,0:T(8,128)(2,1)} %reduce-scatter.2.cloned.1.call-done, bf16[1,640,384]{2,1,0:T(8,128)(2,1)S(1)} %copy-done.3, f32[]{:T(128)} %bitcast.11, f32[]{:T(128)} %bitcast.9, bf16[1,640,384]{2,1,0:T(8,128)(2,1)S(1)} %copy-done.4, ...), kind=kLoop, calls=%fused_computation.25 | loop fusion | flops 5406720 | bytes 3440648 | tf_op jit(solution)/shard_map/broadcast_in_dim | solution.py:116
  219.2 24.9 %conditional.4 = (bf16[640,384]{1,0:T(8,128)(2,1)}) conditional(s32[]{:T(128)} %clamp.3, bf16[640,384]{1,0:T(8,128)(2,1)S(1)} %get-tuple-element.23, bf16[640,384]{1,0:T(8,128)(2,1)S(1)} %get-tuple-element.23, bf16[640,384]{1,0:T(8,128)(2,1)S(1)} %get-tuple-element.23, ...), branch_computations={%region_5.6_spmd, %region_6.7_spmd, %region_7.8_spmd, %region_8.9_... | conditional | bytes 1966128
  219.2 1.9 collective-permute-start.3
  221.1 23.0 %collective-permute-done.3 = bf16[640,384]{1,0:T(8,128)(2,1)} collective-permute-done((bf16[640,384]{1,0:T(8,128)(2,1)S(1)}, bf16[640,384]{1,0:T(8,128)(2,1)}, u32[]{:S(2)}, u32[]{:S(2)}) %collective-permute-start.3) | collective-permute-done | bytes 491552 | tf_op jit(solution)/shard_map/cond/branch_3_fun/ppermute | solution.py:18
  244.0 2.0 fusion.20
  (5 shorter events, 0.0 us)
Async XLA Ops:
  7.2 106.3 %copy-start = (bf16[1,192,128]{2,1,0:T(8,128)(2,1)S(1)}, bf16[1,192,128]{2,1,0:T(8,128)(2,1)}, u32[]{:S(2)}) copy-start(bf16[1,192,128]{2,1,0:T(8,128)(2,1)} %param.19) | copy-start | bytes 147460
  7.2 101.3 %all-gather.3.cloned.1.call-start = ((), (), s32[]{:S(2)}) async-start(), calls=%async_computation.2 | async-start | bytes 4423680 | tf_op jit(solution)/shard_map/all_gather | solution.py:92
  7.9 208.3 %reduce-scatter.2.cloned.1.call-start = ((), (), s32[]{:S(2)}) async-start(), calls=%async_computation.1 | async-start | bytes 4423680 | tf_op jit(solution)/shard_map/reduce_scatter | solution.py:98
  10.0 103.0 %copy-start.5 = (s32[1,192]{1,0:T(1,128)S(1)}, s32[1,192]{1,0:T(1,128)}, u32[]{:S(2)}) copy-start(s32[1,192]{1,0:T(1,128)} %param.14) | copy-start | bytes 2308
  112.5 3.0 %copy-start.2 = (bf16[1,192,5120]{2,1,0:T(8,128)(2,1)S(1)}, bf16[1,192,5120]{2,1,0:T(8,128)(2,1)}, u32[]{:S(2)}) copy-start(bf16[1,192,5120]{2,1,0:T(8,128)(2,1)} %param.13) | copy-start | bytes 5898244
  119.0 97.2 %copy-start.1 = (bf16[1,640,384]{2,1,0:T(8,128)(2,1)S(1)}, bf16[1,640,384]{2,1,0:T(8,128)(2,1)}, u32[]{:S(2)}) copy-start(bf16[1,640,384]{2,1,0:T(8,128)(2,1)} %param.16) | copy-start | bytes 1474564
  119.1 97.2 %copy-start.3 = (bf16[1,640,384]{2,1,0:T(8,128)(2,1)S(1)}, bf16[1,640,384]{2,1,0:T(8,128)(2,1)}, u32[]{:S(2)}) copy-start(bf16[1,640,384]{2,1,0:T(8,128)(2,1)} %param.18) | copy-start | bytes 1474564
  119.1 97.2 %copy-start.4 = (bf16[1,640,384]{2,1,0:T(8,128)(2,1)S(1)}, bf16[1,640,384]{2,1,0:T(8,128)(2,1)}, u32[]{:S(2)}) copy-start(bf16[1,640,384]{2,1,0:T(8,128)(2,1)} %param.17) | copy-start | bytes 1474564
  219.2 24.9 %collective-permute-start.3 = (bf16[640,384]{1,0:T(8,128)(2,1)S(1)}, bf16[640,384]{1,0:T(8,128)(2,1)}, u32[]{:S(2)}, u32[]{:S(2)}) collective-permute-start(bf16[640,384]{1,0:T(8,128)(2,1)S(1)} %param.3), channel_id=1, source_target_pairs={{0,64},{8,72},{16,80},{24,88},{32,96},{40,104},{48,112},{56,120},{... | collective-permute-start | bytes 1474568 | tf_op jit(solution)/shard_map/cond/branch_3_fun/ppermute | solution.py:18
Sparse Core Ops, SparseCore 0:
  10.1 98.3 all-gather.2
  119.2 97.0 reduce-scatter.1
where the time goes:
time: 253 us
  waiting for transfers between devices  218 us (86%)
  between operations  15 us (6%)
  matrix products  9.31 us (4%)
  other arithmetic  8.01 us (3%)
    all_gather x1, waiting for transfers between devices, per_device(): lax.all_gather(local_rows, 'fsdp', axis=0, tiled=True)  98.5 us
    reduce_scatter x1, waiting for transfers between devices, per_device(): lax.psum_scatter(lax.dot_general(features, proj_grad, (((0,), (0,)), ((),...  96.3 us
    ppermute x1, waiting for transfers between devices, partner(): lax.ppermute(value, axis, [(i, i ^ 1 << distance) for i in range(lax.axis...  23 us
  transfers between devices with their start and end apart: 3, of which 3 were waited for; matrix products, arithmetic and copies ran while one was open for 1% of the time, Pallas kernels for 0%

commit v1 on v0

v1 whole, which is shorter than its diff:
```python
import functools

import jax
import jax.numpy as jnp
import numpy as np
from jax import lax
from jax.experimental import pallas as pl
from jax.experimental.pallas import tpu as pltpu
from jax.sharding import PartitionSpec as P

BETA_ONE = 0.9
BETA_TWO = 0.95
LEARN_RATE = 0.002
DECAY_RATE = 0.1
ADAM_EPS = 1e-08

MESH = pl.DeviceIdType.MESH
F32 = jnp.float32
BF16 = jnp.bfloat16
STAGES = 4


def rotary_tables(length, head_dim):
    position = np.arange(length, dtype=np.float32)
    inverse = np.float32(10000.0) ** (-(np.arange(head_dim // 2, dtype=np.float32) * np.float32(2.0 / head_dim)))
    angles = (position[:, None] * inverse[None, :]).astype(np.float32)
    cosine, sine = np.cos(angles), np.sin(angles)
    return np.concatenate([cosine, cosine, -sine, sine], axis=1).astype(np.float32)


def dot(a, b, contract, precision=None):
    return lax.dot_general(a, b, ((contract[0], contract[1]), ((), ())), precision=precision, preferred_element_type=F32)


def attention_grad(projected, doc_row, tables, out_grad):
    length, width = projected.shape
    hd = width // 3
    high = lax.Precision.HIGHEST
    cosine, sine = tables[:, :hd], tables[:, hd:]

    def rotate(x):
        return x * cosine + pltpu.roll(x, hd // 2, 1) * sine

    def rotate_back(x):
        return x * cosine - pltpu.roll(x, hd // 2, 1) * sine

    query = rotate(projected[:, :hd].astype(F32))
    keys = rotate(projected[:, hd : 2 * hd].astype(F32))
    values = projected[:, 2 * hd :]
    rows = lax.broadcasted_iota(jnp.int32, (length, length), 0)
    columns = lax.broadcasted_iota(jnp.int32, (length, length), 1)
    doc_wide = jnp.broadcast_to(doc_row.astype(F32), (length, length))
    doc_col = jnp.sum(jnp.where(rows == columns, doc_wide, 0.0), axis=1, keepdims=True)
    allowed = (columns <= rows) & (doc_wide == doc_col)
    scale = hd ** (-0.5)
    scores = dot(query, keys, ((1,), (1,)), high) * scale
    scores = jnp.where(allowed, scores, -1e30)
    expo = jnp.exp(scores - jnp.max(scores, axis=1, keepdims=True))
    probs = expo / jnp.sum(expo, axis=1, keepdims=True)
    probs_low = probs.astype(BF16)
    grad_values = dot(probs_low, out_grad, ((0,), (0,)))
    grad_probs = dot(out_grad, values, ((1,), (1,)))
    inner = jnp.sum(grad_probs * probs, axis=1, keepdims=True)
    grad_scores = probs * (grad_probs - inner) * scale
    grad_query = rotate_back(dot(grad_scores, keys, ((1,), (0,)), high))
    grad_keys = rotate_back(dot(grad_scores, query, ((0,), (0,)), high))
    return grad_query.astype(BF16), grad_keys.astype(BF16), grad_values.astype(BF16)


def kernel(
    bit, hops,
    coef_ref, doc_ref, tab_ref, act_hbm, w_hbm, first_hbm, second_hbm, og_hbm,
    mixed_hbm, first_out, second_out,
    act_v, xs, xsend, xt, wall, pacc, precv, g_ref, topp, tright, tleft, ropp_l, ropp_r, rleft, rright,
    first_v, second_v, og_v, upd, prt, mix_v, first_o, second_o,
    loc_sem, out_sem, ag_send, ag_recv, x_send, x_recv, p_send, p_recv,
    opp_send, opp_recv, rs_send, rs_recv, sw_send, sw_recv,
):
    rep = lax.axis_index("rep")
    own = lax.axis_index("fsdp")
    z, core = own // 2, own % 2
    right = (rep, ((z + 1) % hops) * 2 + core)
    left = (rep, ((z + hops - 1) % hops) * 2 + core)
    sibling = (rep, z * 2 + (1 - core))
    distance = 2**bit
    partner = (rep + (1 - 2 * ((rep // distance) % 2)) * distance, own)
    seq, width = act_v.shape
    depth, cols = wall.shape[1:]
    half = depth // 2
    chunk = half // STAGES

    def remote(src, dst, send, recv, device):
        return pltpu.make_async_remote_copy(
            src_ref=src, dst_ref=dst, send_sem=send, recv_sem=recv, device_id=device, device_id_type=MESH
        )

    load_act = pltpu.make_async_copy(act_hbm, act_v, loc_sem.at[0])
    load_w = pltpu.make_async_copy(w_hbm, wall.at[0], loc_sem.at[1])
    load_first = pltpu.make_async_copy(first_hbm, first_v, loc_sem.at[2])
    load_second = pltpu.make_async_copy(second_hbm, second_v, loc_sem.at[3])
    load_og = pltpu.make_async_copy(og_hbm, og_v, loc_sem.at[4])
    for load in (load_act, load_w, load_first, load_second, load_og):
        load.start()

    barrier = pltpu.get_barrier_semaphore()
    for device in (right, left, sibling, partner):
        pl.semaphore_signal(barrier, inc=1, device_id=device, device_id_type=MESH)
    pl.semaphore_wait(barrier, 4)

    upper, lower = pl.ds(0, half), pl.ds(half, half)
    gathers = [
        remote(w_hbm.at[upper], wall.at[3, upper], ag_send.at[0], ag_recv.at[0], right),
        remote(w_hbm.at[lower], wall.at[1, lower], ag_send.at[1], ag_recv.at[1], left),
        remote(w_hbm.at[lower], wall.at[3, lower], ag_send.at[2], ag_recv.at[2], right),
        remote(w_hbm.at[upper], wall.at[1, upper], ag_send.at[3], ag_recv.at[3], left),
    ]
    forwards = [
        remote(wall.at[3, upper], wall.at[2, upper], ag_send.at[4], ag_recv.at[4], right),
        remote(wall.at[1, lower], wall.at[2, lower], ag_send.at[5], ag_recv.at[5], left),
    ]
    for copy in gathers:
        copy.start()

    load_act.wait()
    step_rows = 32

    def norm_rows(i, carry):
        rows = pl.ds(pl.multiple_of(i * step_rows, step_rows), step_rows)
        values = act_v[rows, :].astype(F32)
        scale = lax.rsqrt(jnp.sum(values * values, axis=-1, keepdims=True) * (1.0 / width) + 1e-05)
        for d in range(hops):
            block = ((z + d) % hops) * 2
            mine = pl.ds(pl.multiple_of((block + core) * depth, 128), depth)
            other = pl.ds(pl.multiple_of((block + 1 - core) * depth, 128), depth)
            xs[d, rows, :] = (act_v[rows, mine].astype(F32) * scale).astype(BF16)
            xsend[d, rows, :] = (act_v[rows, other].astype(F32) * scale).astype(BF16)
        return carry

    lax.fori_loop(0, seq // step_rows, norm_rows, 0)
    trades = [
        remote(xsend.at[d], xs.at[d, pl.ds(seq, seq)], x_send.at[d], x_recv.at[d], sibling) for d in range(hops)
    ]
    for copy in trades:
        copy.start()
    for copy in trades:
        copy.wait()
    load_w.wait()

    def turn(d, carry):
        xt[d] = xs[d].T
        return carry

    lax.fori_loop(0, hops, turn, 0)

    pacc[...] = dot(xs[0], wall[0], ((1,), (0,)))
    gathers[0].wait_recv()
    forwards[0].start()
    gathers[1].wait_recv()
    forwards[1].start()
    gathers[2].wait_recv()
    pacc[...] += dot(xs[3], wall[3], ((1,), (0,)))
    gathers[3].wait_recv()
    pacc[...] += dot(xs[1], wall[1], ((1,), (0,)))
    for copy in forwards:
        copy.wait_recv()
    pacc[...] += dot(xs[2], wall[2], ((1,), (0,)))

    give = remote(pacc.at[pl.ds(seq, seq)], precv, p_send.at[0], p_recv.at[0], sibling)
    give.start()
    load_og.wait()
    give.wait_recv()
    projected = (pacc[:seq, :] + precv[...]).astype(BF16)
    grads = attention_grad(projected, doc_ref[...], tab_ref[...], og_v[...])
    hd = cols // 3
    for n, part in enumerate(grads):
        g_ref[:seq, n * hd : (n + 1) * hd] = part
    give_g = remote(g_ref.at[pl.ds(0, seq)], g_ref.at[pl.ds(seq, seq)], p_send.at[1], p_recv.at[1], sibling)
    give_g.start()
    give_g.wait_recv()

    def rows_of(i, low):
        return pl.ds(pl.multiple_of(i * chunk + low * half, 16), chunk)

    def part_of(i):
        return pl.ds(pl.multiple_of(i * chunk, 16), chunk)

    def term(d, rows):
        return dot(xt[d, rows, :], g_ref[...], ((1,), (0,)))

    def opp_copy(i, low):
        rows = rows_of(i, low)
        if low:
            return remote(topp.at[rows], ropp_r.at[part_of(i)], opp_send.at[1, i], opp_recv.at[1, i], left)
        return remote(topp.at[rows], ropp_l.at[part_of(i)], opp_send.at[0, i], opp_recv.at[0, i], right)

    def rs_copy(i, low, way):
        rows = rows_of(i, low)
        if way:
            return remote(tleft.at[rows], rright.at[rows], rs_send.at[1, low, i], rs_recv.at[1, low, i], left)
        return remote(tright.at[rows], rleft.at[rows], rs_send.at[0, low, i], rs_recv.at[0, low, i], right)

    def swap_copy(i, low):
        rows = rows_of(i, low)
        return remote(upd.at[rows], prt.at[rows], sw_send.at[low, i], sw_recv.at[low, i], partner)

    def out_copies(i, low):
        rows = rows_of(i, low)
        return [
            pltpu.make_async_copy(first_o.at[rows], first_out.at[rows], out_sem.at[0, low, i]),
            pltpu.make_async_copy(second_o.at[rows], second_out.at[rows], out_sem.at[1, low, i]),
        ]

    def mix_copy(i, low):
        rows = rows_of(i, low)
        return pltpu.make_async_copy(mix_v.at[rows], mixed_hbm.at[rows], out_sem.at[2, low, i])

    def send_opposite(i, carry):
        for low in (0, 1):
            rows = rows_of(i, low)
            topp[rows, :] = term(2, rows).astype(BF16)
            opp_copy(i, low).start()
        return carry

    lax.fori_loop(0, STAGES, send_opposite, 0)

    def send_near(i, carry):
        up, down = rows_of(i, 0), rows_of(i, 1)
        tright[down, :] = term(1, down).astype(BF16)
        rs_copy(i, 1, 0).start()
        tleft[up, :] = term(3, up).astype(BF16)
        rs_copy(i, 0, 1).start()
        opp_copy(i, 0).wait_recv()
        tright[up, :] = (term(1, up) + ropp_l[part_of(i), :].astype(F32)).astype(BF16)
        rs_copy(i, 0, 0).start()
        opp_copy(i, 1).wait_recv()
        tleft[down, :] = (term(3, down) + ropp_r[part_of(i), :].astype(F32)).astype(BF16)
        rs_copy(i, 1, 1).start()
        return carry

    lax.fori_loop(0, STAGES, send_near, 0)

    load_first.wait()
    load_second.wait()
    fix_one, fix_two = coef_ref[0], coef_ref[1]

    def update(i, carry):
        for low in (0, 1):
            rows = rows_of(i, low)
            grad = term(0, rows)
            rs_copy(i, low, 0).wait_recv()
            rs_copy(i, low, 1).wait_recv()
            grad = grad + rleft[rows, :].astype(F32) + rright[rows, :].astype(F32)
            weights = wall[0, rows, :].astype(F32)
            first_new = BETA_ONE * first_v[rows, :].astype(F32) + (1.0 - BETA_ONE) * grad
            second_new = BETA_TWO * second_v[rows, :].astype(F32) + (1.0 - BETA_TWO) * grad * grad
            first_hat = first_new / fix_one
            second_hat = second_new / fix_two
            updated = weights - LEARN_RATE * (first_hat / (jnp.sqrt(second_hat) + ADAM_EPS) + DECAY_RATE * weights)
            upd[rows, :] = updated.astype(BF16)
            swap_copy(i, low).start()
            first_o[rows, :] = first_new.astype(BF16)
            second_o[rows, :] = second_new.astype(BF16)
            for copy in out_copies(i, low):
                copy.start()
        return carry

    def mix(i, carry):
        for low in (0, 1):
            rows = rows_of(i, low)
            swap_copy(i, low).wait_recv()
            mix_v[rows, :] = ((upd[rows, :].astype(F32) + prt[rows, :].astype(F32)) * 0.5).astype(BF16)
            mix_copy(i, low).start()
        return carry

    def update_and_mix(i, carry):
        update(i, carry)
        return mix(i - 1, carry)

    update(0, 0)
    lax.fori_loop(1, STAGES, update_and_mix, 0)
    mix(STAGES - 1, 0)

    for copy in gathers + forwards:
        copy.wait_send()
    give.wait_send()
    give_g.wait_send()

    def finish(i, carry):
        for low in (0, 1):
            opp_copy(i, low).wait_send()
            rs_copy(i, low, 0).wait_send()
            rs_copy(i, low, 1).wait_send()
            swap_copy(i, low).wait_send()
            for copy in out_copies(i, low):
                copy.wait()
            mix_copy(i, low).wait()
        return carry

    lax.fori_loop(0, STAGES, finish, 0)


def per_device(activations, doc_ids, step_index, proj_weights, first_moment, second_moment, out_grad):
    hops = lax.axis_size("fsdp") // 2
    seq, width = activations.shape[1:]
    depth, cols = proj_weights.shape[1:]
    half = depth // 2
    count = (step_index[0] + 1).astype(F32)
    coef = jnp.stack([1.0 - jnp.power(BETA_ONE, count), 1.0 - jnp.power(BETA_TWO, count)])
    tables = jnp.asarray(rotary_tables(seq, cols // 3))
    dma, vmem = pltpu.SemaphoreType.DMA, pltpu.VMEM
    row_block = jax.ShapeDtypeStruct((depth, cols), BF16)

    def branch(bit):
        return pl.pallas_call(
            functools.partial(kernel, bit, hops),
            out_shape=(row_block, row_block, row_block),
            in_specs=[
                pl.BlockSpec(memory_space=pltpu.SMEM),
                pl.BlockSpec(memory_space=pltpu.VMEM),
                pl.BlockSpec(memory_space=pltpu.VMEM),
            ]
            + [pl.BlockSpec(memory_space=pl.ANY)] * 5,
            out_specs=(pl.BlockSpec(memory_space=pl.ANY),) * 3,
            scratch_shapes=[
                vmem((seq, width), BF16),
                vmem((hops, 2 * seq, depth), BF16),
                vmem((hops, seq, depth), BF16),
                vmem((hops, depth, 2 * seq), BF16),
                vmem((hops, depth, cols), BF16),
                vmem((2 * seq, cols), F32),
                vmem((seq, cols), F32),
                vmem((2 * seq, cols), BF16),
                vmem((depth, cols), BF16),
                vmem((depth, cols), BF16),
                vmem((depth, cols), BF16),
                vmem((half, cols), BF16),
                vmem((half, cols), BF16),
                vmem((depth, cols), BF16),
                vmem((depth, cols), BF16),
                vmem((depth, cols), BF16),
                vmem((depth, cols), BF16),
                vmem((seq, cols // 3), BF16),
                vmem((depth, cols), BF16),
                vmem((depth, cols), BF16),
                vmem((depth, cols), BF16),
                vmem((depth, cols), BF16),
                vmem((depth, cols), BF16),
                dma((5,)),
                dma((3, 2, STAGES)),
                dma((6,)),
                dma((6,)),
                dma((hops,)),
                dma((hops,)),
                dma((2,)),
                dma((2,)),
                dma((2, STAGES)),
                dma((2, STAGES)),
                dma((2, 2, STAGES)),
                dma((2, 2, STAGES)),
                dma((2, STAGES)),
                dma((2, STAGES)),
            ],
            compiler_params=pltpu.CompilerParams(
                collective_id=bit, has_side_effects=True, vmem_limit_bytes=40 * 2**20
            ),
        )

    bit_total = lax.axis_size("rep").bit_length() - 1
    outs = lax.switch(
        step_index[0] % bit_total,
        [branch(bit) for bit in range(bit_total)],
        coef, doc_ids, tables, activations[0], proj_weights[0], first_moment[0], second_moment[0], out_grad[0],
    )
    return tuple(out[None] for out in outs)


def solution(mesh):
    rows = P("rep", "fsdp", None)
    return jax.shard_map(
        per_device,
        mesh=mesh,
        in_specs=(rows, P("rep", "fsdp"), P(), rows, rows, rows, rows),
        out_specs=(rows, rows, rows),
        check_vma=False,
    )
```

time: 253 us -> 161 us (0.64)
  the two profiles are of different devices: /device:TPU:1 before, /device:TPU:56 now
where the time goes in v1:
time: 161 us
  Pallas kernels  156 us (97%)
  local copies, waits for them, and re-layouts  2.34 us (1%)
    pallas_call x1, Pallas kernels, per_device(): lax.switch(step_index[0] % bit_total, [branch(bit) for bit in range(bit_t...  156 us

profile of v1, /device:TPU:56, one launch (start us, length us, event | category | flops | bytes accessed | tf_op | source)
XLA Modules:
  0.0 160.6 jit_solution(159558556724136747)
XLA Ops:
  1.4 0.1 pad_maximum_fusion
  1.5 156.8 %conditional.1 = ((bf16[640,384]{1,0:T(8,128)(2,1)S(1)}, bf16[640,384]{1,0:T(8,128)(2,1)S(1)}, bf16[640,384]{1,0:T(8,128)(2,1)S(1)})) conditional(s32[]{:T(128)} %clamp.3, (bf16[1,192,5120]{2,1,0:T(8,128)(2,1)}, bf16[1,640,384]{2,1,0:T(8,128)(2,1)}, bf16[1,640,384]{2,1,0:T(8,128)(2,1)}, ...), branch_computations={%region_0.1_spmd, %region_1.2_spmd, %region_2.3_spmd, %region_3.4_... | conditional | bytes 8 | solution.py:369
  1.5 156.1 %branch_1_fun.1 = (bf16[640,384]{1,0:T(8,128)(2,1)S(1)}, bf16[640,384]{1,0:T(8,128)(2,1)S(1)}, bf16[640,384]{1,0:T(8,128)(2,1)S(1)}) custom-call(f32[2]{0:T(128)S(1)} %get-tuple-element.158.coef_ref, s32[1,192]{1,0:T(1,128)} %get-tuple-element.159.doc_ref, f32[192,256]{1,0:T(8,128)} %get-tuple-element.160.tab_ref, bf16[192,5120]{1,0:T(8,128)(2,1)} %bitcast.35, ...), custom_call_target="tpu_custom_call" | custom-call | tf_op jit(solution)/shard_map/cond/branch_1_fun/pallas_call | solution.py:369
  158.3 0.8 copy.33
  159.1 0.8 copy.34
  159.9 0.8 copy.35

commit v2 on v1

v2 whole, which is shorter than its diff:
```python
import functools

import jax
import jax.numpy as jnp
import numpy as np
from jax import lax
from jax.experimental import pallas as pl
from jax.experimental.pallas import tpu as pltpu
from jax.sharding import PartitionSpec as P

BETA_ONE = 0.9
BETA_TWO = 0.95
LEARN_RATE = 0.002
DECAY_RATE = 0.1
ADAM_EPS = 1e-08

MESH = pl.DeviceIdType.MESH
F32 = jnp.float32
BF16 = jnp.bfloat16
STAGES = 8
PIECES = 2
NORM_ROWS = 32
RUN = 4
PARITY_SHIFT = 1


def rotary_tables(length, head_dim):
    position = np.arange(length, dtype=np.float32)
    inverse = np.float32(10000.0) ** (-(np.arange(head_dim // 2, dtype=np.float32) * np.float32(2.0 / head_dim)))
    angles = (position[:, None] * inverse[None, :]).astype(np.float32)
    cosine, sine = np.cos(angles), np.sin(angles)
    return np.concatenate([cosine, cosine, -sine, sine], axis=1).astype(np.float32)


def dot(a, b, contract, precision=None):
    return lax.dot_general(a, b, ((contract[0], contract[1]), ((), ())), precision=precision, preferred_element_type=F32)


def attention_grad(projected, allowed, tables, out_grad):
    length, width = projected.shape
    hd = width // 3
    high = lax.Precision.HIGHEST
    cosine, sine = tables[:, :hd], tables[:, hd:]

    def rotate(x):
        return x * cosine + pltpu.roll(x, hd // 2, 1) * sine

    def rotate_back(x):
        return x * cosine - pltpu.roll(x, hd // 2, 1) * sine

    query = rotate(projected[:, :hd].astype(F32))
    keys = rotate(projected[:, hd : 2 * hd].astype(F32))
    values = projected[:, 2 * hd :]
    scale = hd ** (-0.5)
    scores = dot(query, keys, ((1,), (1,)), high) * scale
    scores = jnp.where(allowed, scores, -1e30)
    expo = jnp.exp(scores - jnp.max(scores, axis=1, keepdims=True))
    probs = expo / jnp.sum(expo, axis=1, keepdims=True)
    probs_low = probs.astype(BF16)
    grad_values = dot(probs_low, out_grad, ((0,), (0,)))
    grad_probs = dot(out_grad, values, ((1,), (1,)))
    inner = jnp.sum(grad_probs * probs, axis=1, keepdims=True)
    grad_scores = probs * (grad_probs - inner) * scale
    grad_query = rotate_back(dot(grad_scores, keys, ((1,), (0,)), high))
    grad_keys = rotate_back(dot(grad_scores, query, ((0,), (0,)), high))
    return grad_query.astype(BF16), grad_keys.astype(BF16), grad_values.astype(BF16)


def kernel(
    bit, hops,
    coef_ref, doc_ref, tab_ref, act_hbm, w_hbm, first_hbm, second_hbm, og_hbm,
    mixed_hbm, first_out, second_out,
    act_v, xkeep, xaway, skeep, saway, xt, wall, mask, pacc, part_own, part_pair, psend, pz, g_ref,
    tsend, trecv, first_v, second_v, og_v, upd, prt, mix_v, first_o, second_o,
    loc_sem, out_sem, w_sem, x_send, x_recv, p_send, p_recv, g_send, g_recv, rs_send, rs_recv, sw_send, sw_recv,
):
    rep = lax.axis_index("rep")
    own = lax.axis_index("fsdp")
    z, core = own // 2, own % 2
    parity = ((rep // RUN) % hops + PARITY_SHIFT) // 2 % 2
    step = 1 - 2 * ((z + parity) % 2)
    pair_z, next_z, far_z = (z + step + hops) % hops, (z - step + hops) % hops, (z + 2) % hops
    pair = (rep, pair_z * 2 + core)
    following = (rep, next_z * 2 + core)
    sibling = (rep, z * 2 + (1 - core))
    distance = 2**bit
    partner = (rep + (1 - 2 * ((rep // distance) % 2)) * distance, own)
    seq, width = act_v.shape
    depth, cols = wall.shape[1:]
    chunk = depth // STAGES
    hd = cols // 3

    def remote(src, dst, send, recv, device):
        return pltpu.make_async_remote_copy(
            src_ref=src, dst_ref=dst, send_sem=send, recv_sem=recv, device_id=device, device_id_type=MESH
        )

    load_act = pltpu.make_async_copy(act_hbm, act_v, loc_sem.at[0])
    load_w = pltpu.make_async_copy(w_hbm, wall.at[0], loc_sem.at[1])
    load_first = pltpu.make_async_copy(first_hbm, first_v, loc_sem.at[2])
    load_second = pltpu.make_async_copy(second_hbm, second_v, loc_sem.at[3])
    load_og = pltpu.make_async_copy(og_hbm, og_v, loc_sem.at[4])
    for load in (load_act, load_w, load_first, load_second, load_og):
        load.start()

    barrier = pltpu.get_barrier_semaphore()
    for device in (pair, following, sibling, partner):
        pl.semaphore_signal(barrier, inc=1, device_id=device, device_id_type=MESH)
    pl.semaphore_wait(barrier, 4)

    send_w = remote(w_hbm, wall.at[1], w_sem.at[0], w_sem.at[1], following)
    send_w.start()

    load_act.wait()
    piece = seq // PIECES

    def rows_at(base, c):
        return pl.ds(pl.multiple_of(base + c * piece, 16), piece)

    def trade_away(c):
        return remote(saway.at[:, rows_at(0, c)], xaway.at[:, rows_at(seq, c)], x_send.at[0, c], x_recv.at[0, c], sibling)

    def trade_keep(c):
        return remote(skeep.at[:, rows_at(0, c)], xkeep.at[:, rows_at(seq, c)], x_send.at[1, c], x_recv.at[1, c], sibling)

    def pair_own(c):
        return remote(xaway.at[:, rows_at(0, c)], xkeep.at[:, rows_at(2 * seq, c)], x_send.at[2, c], x_recv.at[2, c], pair)

    def pair_sibling(c):
        return remote(xaway.at[:, rows_at(seq, c)], xkeep.at[:, rows_at(3 * seq, c)], x_send.at[3, c], x_recv.at[3, c], pair)

    def norm_piece(c, carry):
        def norm_rows(i, inner):
            rows = pl.ds(pl.multiple_of(c * piece + i * NORM_ROWS, 16), NORM_ROWS)
            values = act_v[rows, :].astype(F32)
            scale = lax.rsqrt(jnp.sum(values * values, axis=-1, keepdims=True) * (1.0 / width) + 1e-05)
            for block_z, mine, other, slot in (
                (pair_z, xaway, saway, 0), (far_z, xaway, saway, 1), (z, xkeep, skeep, 0), (next_z, xkeep, skeep, 1),
            ):
                here = pl.ds(pl.multiple_of((block_z * 2 + core) * depth, 128), depth)
                there = pl.ds(pl.multiple_of((block_z * 2 + 1 - core) * depth, 128), depth)
                mine[slot, rows, :] = (act_v[rows, here].astype(F32) * scale).astype(BF16)
                other[slot, rows, :] = (act_v[rows, there].astype(F32) * scale).astype(BF16)
            return inner

        lax.fori_loop(0, piece // NORM_ROWS, norm_rows, 0)
        pair_own(c).start()
        trade_away(c).start()
        trade_keep(c).start()
        return carry

    lax.fori_loop(0, PIECES, norm_piece, 0)
    for c in range(PIECES):
        trade_away(c).wait_recv()
        pair_sibling(c).start()

    rows = lax.broadcasted_iota(jnp.int32, (seq, seq), 0)
    columns = lax.broadcasted_iota(jnp.int32, (seq, seq), 1)
    doc_wide = jnp.broadcast_to(doc_ref[...].astype(F32), (seq, seq))
    doc_col = jnp.sum(jnp.where(rows == columns, doc_wide, 0.0), axis=1, keepdims=True)
    mask[...] = jnp.where((columns <= rows) & (doc_wide == doc_col), 1.0, 0.0)

    for c in range(PIECES):
        trade_keep(c).wait_recv()
    near, far = pl.ds(0, 2 * seq), pl.ds(2 * seq, 2 * seq)

    def turn(slot, base, count):
        xt[slot, :, base : base + count] = xkeep[slot, base : base + count, :].T

    for slot in (0, 1):
        turn(slot, 0, 2 * seq)
    load_w.wait()
    send_w.wait_recv()

    def project(base, count):
        part = pl.ds(base, count)
        pacc[part, :] = dot(xkeep[0, part, :], wall[0], ((1,), (0,))) + dot(xkeep[1, part, :], wall[1], ((1,), (0,)))

    project(0, 2 * seq)
    give_own = remote(pacc.at[pl.ds(seq, seq)], part_own, p_send.at[0], p_recv.at[0], sibling)
    give_own.start()
    for c in range(PIECES):
        pair_own(c).wait_recv()
    project(2 * seq, seq)
    for c in range(PIECES):
        pair_sibling(c).wait_recv()
    project(3 * seq, seq)
    give_pair = remote(pacc.at[pl.ds(3 * seq, seq)], part_pair, p_send.at[1], p_recv.at[1], sibling)
    give_pair.start()
    give_pair.wait_recv()
    psend[...] = (pacc[2 * seq : 3 * seq, :] + part_pair[...]).astype(BF16)
    give_back = remote(psend, pz, p_send.at[2], p_recv.at[2], pair)
    give_back.start()
    for slot in (0, 1):
        turn(slot, 2 * seq, 2 * seq)
    load_og.wait()
    give_own.wait_recv()
    give_back.wait_recv()
    projected = (pacc[:seq, :] + part_own[...] + pz[...].astype(F32)).astype(BF16)
    grads = attention_grad(projected, mask[...] > 0.5, tab_ref[...], og_v[...])
    for n, grad_part in enumerate(grads):
        g_ref[:seq, n * hd : (n + 1) * hd] = grad_part
    g_pair = remote(g_ref.at[pl.ds(0, seq)], g_ref.at[pl.ds(2 * seq, seq)], g_send.at[0], g_recv.at[0], pair)
    g_sibling = remote(g_ref.at[pl.ds(0, seq)], g_ref.at[pl.ds(seq, seq)], g_send.at[1], g_recv.at[1], sibling)
    g_on = remote(g_ref.at[pl.ds(2 * seq, seq)], g_ref.at[pl.ds(3 * seq, seq)], g_send.at[2], g_recv.at[2], sibling)
    g_pair.start()
    g_sibling.start()
    g_pair.wait_recv()
    g_on.start()
    g_sibling.wait_recv()
    g_on.wait_recv()

    def rows_of(i):
        return pl.ds(pl.multiple_of(i * chunk, 16), chunk)

    def term(slot, rows):
        return dot(xt[slot, rows, :], g_ref[...], ((1,), (0,)))

    def rs_copy(i):
        return remote(tsend.at[rows_of(i)], trecv.at[rows_of(i)], rs_send.at[i], rs_recv.at[i], following)

    def swap_copy(i):
        return remote(upd.at[rows_of(i)], prt.at[rows_of(i)], sw_send.at[i], sw_recv.at[i], partner)

    def out_copies(i):
        return [
            pltpu.make_async_copy(first_o.at[rows_of(i)], first_out.at[rows_of(i)], out_sem.at[0, i]),
            pltpu.make_async_copy(second_o.at[rows_of(i)], second_out.at[rows_of(i)], out_sem.at[1, i]),
        ]

    def mix_copy(i):
        return pltpu.make_async_copy(mix_v.at[rows_of(i)], mixed_hbm.at[rows_of(i)], out_sem.at[2, i])

    def send_terms(i, carry):
        tsend[rows_of(i), :] = term(1, rows_of(i)).astype(BF16)
        rs_copy(i).start()
        return carry

    lax.fori_loop(0, STAGES, send_terms, 0)

    load_first.wait()
    load_second.wait()
    fix_one, fix_two = coef_ref[0], coef_ref[1]

    def update(i, carry):
        rows = rows_of(i)
        grad = term(0, rows)
        rs_copy(i).wait_recv()
        grad = grad + trecv[rows, :].astype(F32)
        weights = wall[0, rows, :].astype(F32)
        first_new = BETA_ONE * first_v[rows, :].astype(F32) + (1.0 - BETA_ONE) * grad
        second_new = BETA_TWO * second_v[rows, :].astype(F32) + (1.0 - BETA_TWO) * grad * grad
        first_hat = first_new / fix_one
        second_hat = second_new / fix_two
        updated = weights - LEARN_RATE * (first_hat / (jnp.sqrt(second_hat) + ADAM_EPS) + DECAY_RATE * weights)
        upd[rows, :] = updated.astype(BF16)
        swap_copy(i).start()
        first_o[rows, :] = first_new.astype(BF16)
        second_o[rows, :] = second_new.astype(BF16)
        for copy in out_copies(i):
            copy.start()
        return carry

    def mix(i, carry):
        rows = rows_of(i)
        swap_copy(i).wait_recv()
        mix_v[rows, :] = ((upd[rows, :].astype(F32) + prt[rows, :].astype(F32)) * 0.5).astype(BF16)
        mix_copy(i).start()
        return carry

    def update_and_mix(i, carry):
        update(i, carry)
        return mix(i - 1, carry)

    update(0, 0)
    lax.fori_loop(1, STAGES, update_and_mix, 0)
    mix(STAGES - 1, 0)

    for copy in (send_w, give_own, give_pair, give_back, g_pair, g_sibling, g_on):
        copy.wait_send()
    for c in range(PIECES):
        for copy in (trade_away(c), trade_keep(c), pair_own(c), pair_sibling(c)):
            copy.wait_send()

    def finish(i, carry):
        rs_copy(i).wait_send()
        swap_copy(i).wait_send()
        for copy in out_copies(i):
            copy.wait()
        mix_copy(i).wait()
        return carry

    lax.fori_loop(0, STAGES, finish, 0)


def per_device(activations, doc_ids, step_index, proj_weights, first_moment, second_moment, out_grad):
    hops = lax.axis_size("fsdp") // 2
    seq, width = activations.shape[1:]
    depth, cols = proj_weights.shape[1:]
    count = (step_index[0] + 1).astype(F32)
    coef = jnp.stack([1.0 - jnp.power(BETA_ONE, count), 1.0 - jnp.power(BETA_TWO, count)])
    tables = jnp.asarray(rotary_tables(seq, cols // 3))
    dma, vmem = pltpu.SemaphoreType.DMA, pltpu.VMEM
    row_vmem = vmem((depth, cols), BF16)
    row_block = jax.ShapeDtypeStruct((depth, cols), BF16)

    def branch(bit):
        return pl.pallas_call(
            functools.partial(kernel, bit, hops),
            out_shape=(row_block, row_block, row_block),
            in_specs=[
                pl.BlockSpec(memory_space=pltpu.SMEM),
                pl.BlockSpec(memory_space=pltpu.VMEM),
                pl.BlockSpec(memory_space=pltpu.VMEM),
            ]
            + [pl.BlockSpec(memory_space=pl.ANY)] * 5,
            out_specs=(pl.BlockSpec(memory_space=pl.ANY),) * 3,
            scratch_shapes=[
                vmem((seq, width), BF16),
                vmem((2, 4 * seq, depth), BF16),
                vmem((2, 2 * seq, depth), BF16),
                vmem((2, seq, depth), BF16),
                vmem((2, seq, depth), BF16),
                vmem((2, depth, 4 * seq), BF16),
                vmem((2, depth, cols), BF16),
                vmem((seq, seq), F32),
                vmem((4 * seq, cols), F32),
                vmem((seq, cols), F32),
                vmem((seq, cols), F32),
                vmem((seq, cols), BF16),
                vmem((seq, cols), BF16),
                vmem((4 * seq, cols), BF16),
                row_vmem,
                row_vmem,
                row_vmem,
                row_vmem,
                vmem((seq, cols // 3), BF16),
                row_vmem,
                row_vmem,
                row_vmem,
                row_vmem,
                row_vmem,
                dma((5,)),
                dma((3, STAGES)),
                dma((2,)),
                dma((4, PIECES)),
                dma((4, PIECES)),
                dma((3,)),
                dma((3,)),
                dma((3,)),
                dma((3,)),
                dma((STAGES,)),
                dma((STAGES,)),
                dma((STAGES,)),
                dma((STAGES,)),
            ],
            compiler_params=pltpu.CompilerParams(
                collective_id=bit, has_side_effects=True, vmem_limit_bytes=40 * 2**20
            ),
        )

    bit_total = lax.axis_size("rep").bit_length() - 1
    outs = lax.switch(
        step_index[0] % bit_total,
        [branch(bit) for bit in range(bit_total)],
        coef, doc_ids, tables, activations[0], proj_weights[0], first_moment[0], second_moment[0], out_grad[0],
    )
    return tuple(out[None] for out in outs)


def solution(mesh):
    rows = P("rep", "fsdp", None)
    return jax.shard_map(
        per_device,
        mesh=mesh,
        in_specs=(rows, P("rep", "fsdp"), P(), rows, rows, rows, rows),
        out_specs=(rows, rows, rows),
        check_vma=False,
    )
```

time: 161 us -> 165 us (1.025)
  the two profiles are of different devices: /device:TPU:56 before, /device:TPU:316 now
where the time goes in v2:
time: 165 us
  Pallas kernels  160 us (97%)
  local copies, waits for them, and re-layouts  2.34 us (1%)
    pallas_call x1, Pallas kernels, per_device(): lax.switch(step_index[0] % bit_total, [branch(bit) for bit in range(bit_t...  160 us

profile of v2, /device:TPU:316, one launch (start us, length us, event | category | flops | bytes accessed | tf_op | source)
XLA Modules:
  0.0 164.7 jit_solution(5017302260654410458)
XLA Ops:
  1.4 0.1 pad_maximum_fusion
  1.5 160.9 %conditional.1 = ((bf16[640,384]{1,0:T(8,128)(2,1)S(1)}, bf16[640,384]{1,0:T(8,128)(2,1)S(1)}, bf16[640,384]{1,0:T(8,128)(2,1)S(1)})) conditional(s32[]{:T(128)} %clamp.3, (bf16[1,192,5120]{2,1,0:T(8,128)(2,1)}, bf16[1,640,384]{2,1,0:T(8,128)(2,1)}, bf16[1,640,384]{2,1,0:T(8,128)(2,1)}, ...), branch_computations={%region_0.1_spmd, %region_1.2_spmd, %region_2.3_spmd, %region_3.4_... | conditional | bytes 8 | solution.py:363
  1.5 160.2 %branch_1_fun.1 = (bf16[640,384]{1,0:T(8,128)(2,1)S(1)}, bf16[640,384]{1,0:T(8,128)(2,1)S(1)}, bf16[640,384]{1,0:T(8,128)(2,1)S(1)}) custom-call(f32[2]{0:T(128)S(1)} %get-tuple-element.158.coef_ref, s32[1,192]{1,0:T(1,128)} %get-tuple-element.159.doc_ref, f32[192,256]{1,0:T(8,128)} %get-tuple-element.160.tab_ref, bf16[192,5120]{1,0:T(8,128)(2,1)} %bitcast.35, ...), custom_call_target="tpu_custom_call" | custom-call | tf_op jit(solution)/shard_map/cond/branch_1_fun/pallas_call | solution.py:363
  162.3 0.8 copy.33
  163.1 0.8 copy.34
  163.9 0.8 copy.35

commit v3 on v2

v3 whole, which is shorter than its diff:
```python
import functools

import jax
import jax.numpy as jnp
import numpy as np
from jax import lax
from jax.experimental import pallas as pl
from jax.experimental.pallas import tpu as pltpu
from jax.sharding import PartitionSpec as P

BETA_ONE = 0.9
BETA_TWO = 0.95
LEARN_RATE = 0.002
DECAY_RATE = 0.1
ADAM_EPS = 1e-08

MESH = pl.DeviceIdType.MESH
F32 = jnp.float32
BF16 = jnp.bfloat16
PIECES = 2
NORM_ROWS = 32
PART = 256
CHUNK = 64


def rotary_tables(length, head_dim):
    position = np.arange(length, dtype=np.float32)
    inverse = np.float32(10000.0) ** (-(np.arange(head_dim // 2, dtype=np.float32) * np.float32(2.0 / head_dim)))
    angles = (position[:, None] * inverse[None, :]).astype(np.float32)
    cosine, sine = np.cos(angles), np.sin(angles)
    return np.concatenate([cosine, cosine, -sine, sine], axis=1).astype(np.float32)


def dot(a, b, contract, precision=None):
    return lax.dot_general(a, b, ((contract[0], contract[1]), ((), ())), precision=precision, preferred_element_type=F32)


def attention_grad(projected, allowed, tables, out_grad):
    length, width = projected.shape
    hd = width // 3
    high = lax.Precision.HIGHEST
    cosine, sine = tables[:, :hd], tables[:, hd:]

    def rotate(x):
        return x * cosine + pltpu.roll(x, hd // 2, 1) * sine

    def rotate_back(x):
        return x * cosine - pltpu.roll(x, hd // 2, 1) * sine

    query = rotate(projected[:, :hd].astype(F32))
    keys = rotate(projected[:, hd : 2 * hd].astype(F32))
    values = projected[:, 2 * hd :]
    scale = hd ** (-0.5)
    scores = dot(query, keys, ((1,), (1,)), high) * scale
    scores = jnp.where(allowed, scores, -1e30)
    expo = jnp.exp(scores - jnp.max(scores, axis=1, keepdims=True))
    probs = expo / jnp.sum(expo, axis=1, keepdims=True)
    probs_low = probs.astype(BF16)
    grad_values = dot(probs_low, out_grad, ((0,), (0,)))
    grad_probs = dot(out_grad, values, ((1,), (1,)))
    inner = jnp.sum(grad_probs * probs, axis=1, keepdims=True)
    grad_scores = probs * (grad_probs - inner) * scale
    grad_query = rotate_back(dot(grad_scores, keys, ((1,), (0,)), high))
    grad_keys = rotate_back(dot(grad_scores, query, ((0,), (0,)), high))
    return grad_query.astype(BF16), grad_keys.astype(BF16), grad_values.astype(BF16)


def kernel(
    bit, hops,
    coef_ref, doc_ref, tab_ref, act_hbm, w_hbm, first_hbm, second_hbm, og_hbm,
    mixed_hbm, first_out, second_out,
    act_v, keep0, keep1, away0, away1, skeep0, skeep1, saway0, saway1, xt0, xt1, w_own, w0, w1,
    mask, pacc, pacc0, pacc1, rec, rec0, rec1, psend, pz, g_ref,
    tsend, trecv, first_v, second_v, og_v, upd, prt, mix_v, first_o, second_o,
    loc_sem, out_sem, w_send, w_recv, x_send, x_recv, p_send, p_recv, g_send, g_recv, rs_send, rs_recv, sw_send, sw_recv,
):
    rep = lax.axis_index("rep")
    own = lax.axis_index("fsdp")
    z, core = own // 2, own % 2
    step = 1 - 2 * ((z + core) % 2)
    z0, z1, far = (z + step + hops) % hops, (z - step + hops) % hops, (z + 2) % hops
    side0 = (rep, z0 * 2 + core)
    side1 = (rep, z1 * 2 + core)
    sibling = (rep, z * 2 + (1 - core))
    distance = 2**bit
    partner = (rep + (1 - 2 * ((rep // distance) % 2)) * distance, own)
    seq, width = act_v.shape
    depth, cols = w_own.shape
    depth0, depth1 = w0.shape[0], w1.shape[0]
    hd = cols // 3
    chunks0, chunks1 = depth0 // CHUNK, depth1 // CHUNK

    def remote(src, dst, send, recv, device):
        return pltpu.make_async_remote_copy(
            src_ref=src, dst_ref=dst, send_sem=send, recv_sem=recv, device_id=device, device_id_type=MESH
        )

    load_act = pltpu.make_async_copy(act_hbm, act_v, loc_sem.at[0])
    load_w = pltpu.make_async_copy(w_hbm, w_own, loc_sem.at[1])
    load_first = pltpu.make_async_copy(first_hbm, first_v, loc_sem.at[2])
    load_second = pltpu.make_async_copy(second_hbm, second_v, loc_sem.at[3])
    load_og = pltpu.make_async_copy(og_hbm, og_v, loc_sem.at[4])
    for load in (load_act, load_w, load_first, load_second, load_og):
        load.start()

    barrier = pltpu.get_barrier_semaphore()
    for device in (side0, side1, sibling, partner):
        pl.semaphore_signal(barrier, inc=1, device_id=device, device_id_type=MESH)
    pl.semaphore_wait(barrier, 4)

    send_w0 = remote(w_hbm.at[pl.ds(0, depth0)], w0, w_send.at[0], w_recv.at[0], side1)
    send_w1 = remote(w_hbm.at[pl.ds(depth0, depth1)], w1, w_send.at[1], w_recv.at[1], side0)
    send_w0.start()
    send_w1.start()

    load_act.wait()
    piece = seq // PIECES

    def rows_at(base, c):
        return pl.ds(pl.multiple_of(base + c * piece, 16), piece)

    def to_sibling(n, c):
        src, dst = ((saway0, away0), (saway1, away1), (skeep0, keep0), (skeep1, keep1))[n]
        return remote(src.at[:, rows_at(0, c)], dst.at[:, rows_at(seq, c)], x_send.at[n, c], x_recv.at[n, c], sibling)

    def to_pair(part, second, c):
        src, dst, device = ((away0, keep0, side0), (away1, keep1, side1))[part]
        n = 4 + 2 * part + second
        return remote(
            src.at[:, rows_at(second * seq, c)], dst.at[:, rows_at((2 + second) * seq, c)],
            x_send.at[n, c], x_recv.at[n, c], device,
        )

    mine = ((z, keep0, 0, keep1, 0), (z0, away0, 0, keep1, 1), (z1, keep0, 1, away1, 0), (far, away0, 1, away1, 1))
    other = ((z, skeep0, 0, skeep1, 0), (z0, skeep0, 1, saway1, 0), (z1, saway0, 0, skeep1, 1), (far, saway0, 1, saway1, 1))

    def norm_piece(c, carry):
        def norm_rows(i, inner):
            rows = pl.ds(pl.multiple_of(c * piece + i * NORM_ROWS, 16), NORM_ROWS)
            values = act_v[rows, :].astype(F32)
            scale = lax.rsqrt(jnp.sum(values * values, axis=-1, keepdims=True) * (1.0 / width) + 1e-05)
            for places, which in ((mine, core), (other, 1 - core)):
                for chip, ref0, slot0, ref1, slot1 in places:
                    base = (chip * 2 + which) * depth
                    cols0 = pl.ds(pl.multiple_of(base, 128), depth0)
                    cols1 = pl.ds(pl.multiple_of(base + depth0, 128), depth1)
                    ref0[slot0, rows, :] = (act_v[rows, cols0].astype(F32) * scale).astype(BF16)
                    ref1[slot1, rows, :] = (act_v[rows, cols1].astype(F32) * scale).astype(BF16)
            return inner

        lax.fori_loop(0, piece // NORM_ROWS, norm_rows, 0)
        to_pair(0, 0, c).start()
        to_pair(1, 0, c).start()
        for n in range(4):
            to_sibling(n, c).start()
        return carry

    lax.fori_loop(0, PIECES, norm_piece, 0)
    for c in range(PIECES):
        for part in (0, 1):
            to_sibling(part, c).wait_recv()
            to_pair(part, 1, c).start()

    rows = lax.broadcasted_iota(jnp.int32, (seq, seq), 0)
    columns = lax.broadcasted_iota(jnp.int32, (seq, seq), 1)
    doc_wide = jnp.broadcast_to(doc_ref[...].astype(F32), (seq, seq))
    doc_col = jnp.sum(jnp.where(rows == columns, doc_wide, 0.0), axis=1, keepdims=True)
    mask[...] = jnp.where((columns <= rows) & (doc_wide == doc_col), 1.0, 0.0)

    for c in range(PIECES):
        for n in (2, 3):
            to_sibling(n, c).wait_recv()

    def turn(base):
        for keep, xt in ((keep0, xt0), (keep1, xt1)):
            for slot in (0, 1):
                xt[slot, :, base : base + 2 * seq] = keep[slot, base : base + 2 * seq, :].T

    turn(0)
    load_w.wait()
    send_w0.wait_recv()
    send_w1.wait_recv()
    plain = ((1,), (0,))

    def project0(base, count):
        part = pl.ds(base, count)
        return dot(keep0[0, part, :], w_own[:depth0, :], plain) + dot(keep0[1, part, :], w0[...], plain)

    def project1(base, count):
        part = pl.ds(base, count)
        return dot(keep1[0, part, :], w_own[depth0:, :], plain) + dot(keep1[1, part, :], w1[...], plain)

    pacc[...] = project0(0, 2 * seq) + project1(0, 2 * seq)
    low, high = pl.ds(0, seq), pl.ds(seq, seq)
    give = remote(pacc.at[high], rec, p_send.at[0], p_recv.at[0], sibling)
    give.start()
    for c in range(PIECES):
        to_pair(0, 0, c).wait_recv()
    pacc0[low, :] = project0(2 * seq, seq)
    for c in range(PIECES):
        to_pair(1, 0, c).wait_recv()
    pacc1[low, :] = project1(2 * seq, seq)
    for c in range(PIECES):
        to_pair(0, 1, c).wait_recv()
    pacc0[high, :] = project0(3 * seq, seq)
    give0 = remote(pacc0.at[high], rec1, p_send.at[1], p_recv.at[1], sibling)
    give0.start()
    for c in range(PIECES):
        to_pair(1, 1, c).wait_recv()
    pacc1[high, :] = project1(3 * seq, seq)
    give1 = remote(pacc1.at[high], rec0, p_send.at[2], p_recv.at[2], sibling)
    give1.start()
    give0.wait_recv()
    psend[1] = (pacc1[low, :] + rec1[...]).astype(BF16)
    back1 = remote(psend.at[1], pz.at[1], p_send.at[3], p_recv.at[3], side1)
    back1.start()
    give1.wait_recv()
    psend[0] = (pacc0[low, :] + rec0[...]).astype(BF16)
    back0 = remote(psend.at[0], pz.at[0], p_send.at[4], p_recv.at[4], side0)
    back0.start()
    turn(2 * seq)
    load_og.wait()
    give.wait_recv()
    back0.wait_recv()
    back1.wait_recv()
    projected = (pacc[low, :] + rec[...] + pz[0].astype(F32) + pz[1].astype(F32)).astype(BF16)
    grads = attention_grad(projected, mask[...] > 0.5, tab_ref[...], og_v[...])
    for n, grad_part in enumerate(grads):
        g_ref[:seq, n * hd : (n + 1) * hd] = grad_part

    def g_rows(n):
        return g_ref.at[pl.ds(n * seq, seq)]

    g_copies = [
        remote(g_rows(src), g_rows(dst), g_send.at[n], g_recv.at[n], device)
        for n, (src, dst, device) in enumerate(
            ((0, 2, side0), (0, 4, side1), (0, 1, sibling), (2, 5, sibling), (4, 3, sibling))
        )
    ]
    for n in (0, 1, 2):
        g_copies[n].start()
    g_copies[0].wait_recv()
    g_copies[3].start()
    g_copies[1].wait_recv()
    g_copies[4].start()
    for n in (2, 3, 4):
        g_copies[n].wait_recv()

    def part_rows(i):
        return pl.ds(pl.multiple_of(i * CHUNK, 16), CHUNK)

    def rows_of(part, i):
        return pl.ds(pl.multiple_of(part * depth0 + i * CHUNK, 16), CHUNK)

    def term(slot, part, i):
        if part == 0:
            return dot(xt0[slot, part_rows(i), :], g_ref[: 4 * seq, :], plain)
        return dot(xt1[slot, part_rows(i), : 2 * seq], g_ref[: 2 * seq, :], plain) + dot(
            xt1[slot, part_rows(i), 2 * seq :], g_ref[4 * seq :, :], plain
        )

    def rs_copy(part, i):
        rows = rows_of(part, i)
        device = (side1, side0)[part]
        return remote(tsend.at[rows], trecv.at[rows], rs_send.at[part, i], rs_recv.at[part, i], device)

    def swap_copy(part, i):
        rows = rows_of(part, i)
        return remote(upd.at[rows], prt.at[rows], sw_send.at[part, i], sw_recv.at[part, i], partner)

    def out_copies(part, i):
        rows = rows_of(part, i)
        return [
            pltpu.make_async_copy(first_o.at[rows], first_out.at[rows], out_sem.at[0, part, i]),
            pltpu.make_async_copy(second_o.at[rows], second_out.at[rows], out_sem.at[1, part, i]),
        ]

    def mix_copy(part, i):
        rows = rows_of(part, i)
        return pltpu.make_async_copy(mix_v.at[rows], mixed_hbm.at[rows], out_sem.at[2, part, i])

    def send_term(part, i):
        tsend[rows_of(part, i), :] = term(1, part, i).astype(BF16)
        rs_copy(part, i).start()

    def update(part, i):
        rows = rows_of(part, i)
        grad = term(0, part, i)
        rs_copy(part, i).wait_recv()
        grad = grad + trecv[rows, :].astype(F32)
        weights = w_own[rows, :].astype(F32)
        first_new = BETA_ONE * first_v[rows, :].astype(F32) + (1.0 - BETA_ONE) * grad
        second_new = BETA_TWO * second_v[rows, :].astype(F32) + (1.0 - BETA_TWO) * grad * grad
        first_hat = first_new / coef_ref[0]
        second_hat = second_new / coef_ref[1]
        updated = weights - LEARN_RATE * (first_hat / (jnp.sqrt(second_hat) + ADAM_EPS) + DECAY_RATE * weights)
        upd[rows, :] = updated.astype(BF16)
        swap_copy(part, i).start()
        first_o[rows, :] = first_new.astype(BF16)
        second_o[rows, :] = second_new.astype(BF16)
        for copy in out_copies(part, i):
            copy.start()

    def mix(part, i):
        rows = rows_of(part, i)
        swap_copy(part, i).wait_recv()
        mix_v[rows, :] = ((upd[rows, :].astype(F32) + prt[rows, :].astype(F32)) * 0.5).astype(BF16)
        mix_copy(part, i).start()

    def finish(part, i):
        rs_copy(part, i).wait_send()
        swap_copy(part, i).wait_send()
        for copy in out_copies(part, i):
            copy.wait()
        mix_copy(part, i).wait()

    def over_chunks(*calls):
        def both(i, carry):
            for call in calls:
                call(0, i)
                call(1, i)
            return carry

        def rest(i, carry):
            for call in calls:
                call(1, i)
            return carry

        lax.fori_loop(0, chunks0, both, 0)
        lax.fori_loop(chunks0, chunks1, rest, 0)

    over_chunks(send_term)
    load_first.wait()
    load_second.wait()

    update(0, 0)
    update(1, 0)

    def steady(i, carry):
        update(0, i)
        mix(0, i - 1)
        update(1, i)
        mix(1, i - 1)
        return carry

    def steady_rest(i, carry):
        update(1, i)
        mix(1, i - 1)
        return carry

    lax.fori_loop(1, chunks0, steady, 0)
    mix(0, chunks0 - 1)
    lax.fori_loop(chunks0, chunks1, steady_rest, 0)
    mix(1, chunks1 - 1)

    for copy in [send_w0, send_w1, give, give0, give1, back0, back1] + g_copies:
        copy.wait_send()
    for c in range(PIECES):
        for n in range(4):
            to_sibling(n, c).wait_send()
        for part in (0, 1):
            to_pair(part, 0, c).wait_send()
            to_pair(part, 1, c).wait_send()
    over_chunks(finish)


def per_device(activations, doc_ids, step_index, proj_weights, first_moment, second_moment, out_grad):
    hops = lax.axis_size("fsdp") // 2
    seq, width = activations.shape[1:]
    depth, cols = proj_weights.shape[1:]
    count = (step_index[0] + 1).astype(F32)
    coef = jnp.stack([1.0 - jnp.power(BETA_ONE, count), 1.0 - jnp.power(BETA_TWO, count)])
    tables = jnp.asarray(rotary_tables(seq, cols // 3))
    dma, vmem = pltpu.SemaphoreType.DMA, pltpu.VMEM
    rest = depth - PART
    stages = max(PART, rest) // CHUNK
    row_vmem = vmem((depth, cols), BF16)
    row_block = jax.ShapeDtypeStruct((depth, cols), BF16)

    def branch(bit):
        return pl.pallas_call(
            functools.partial(kernel, bit, hops),
            out_shape=(row_block, row_block, row_block),
            in_specs=[
                pl.BlockSpec(memory_space=pltpu.SMEM),
                pl.BlockSpec(memory_space=pltpu.VMEM),
                pl.BlockSpec(memory_space=pltpu.VMEM),
            ]
            + [pl.BlockSpec(memory_space=pl.ANY)] * 5,
            out_specs=(pl.BlockSpec(memory_space=pl.ANY),) * 3,
            scratch_shapes=[
                vmem((seq, width), BF16),
                vmem((2, 4 * seq, PART), BF16),
                vmem((2, 4 * seq, rest), BF16),
                vmem((2, 2 * seq, PART), BF16),
                vmem((2, 2 * seq, rest), BF16),
                vmem((2, seq, PART), BF16),
                vmem((2, seq, rest), BF16),
                vmem((2, seq, PART), BF16),
                vmem((2, seq, rest), BF16),
                vmem((2, PART, 4 * seq), BF16),
                vmem((2, rest, 4 * seq), BF16),
                row_vmem,
                vmem((PART, cols), BF16),
                vmem((rest, cols), BF16),
                vmem((seq, seq), F32),
                vmem((2 * seq, cols), F32),
                vmem((2 * seq, cols), F32),
                vmem((2 * seq, cols), F32),
                vmem((seq, cols), F32),
                vmem((seq, cols), F32),
                vmem((seq, cols), F32),
                vmem((2, seq, cols), BF16),
                vmem((2, seq, cols), BF16),
                vmem((6 * seq, cols), BF16),
                row_vmem,
                row_vmem,
                row_vmem,
                row_vmem,
                vmem((seq, cols // 3), BF16),
                row_vmem,
                row_vmem,
                row_vmem,
                row_vmem,
                row_vmem,
                dma((5,)),
                dma((3, 2, stages)),
                dma((2,)),
                dma((2,)),
                dma((8, PIECES)),
                dma((8, PIECES)),
                dma((5,)),
                dma((5,)),
                dma((5,)),
                dma((5,)),
                dma((2, stages)),
                dma((2, stages)),
                dma((2, stages)),
                dma((2, stages)),
            ],
            compiler_params=pltpu.CompilerParams(
                collective_id=bit, has_side_effects=True, vmem_limit_bytes=40 * 2**20
            ),
        )

    bit_total = lax.axis_size("rep").bit_length() - 1
    outs = lax.switch(
        step_index[0] % bit_total,
        [branch(bit) for bit in range(bit_total)],
        coef, doc_ids, tables, activations[0], proj_weights[0], first_moment[0], second_moment[0], out_grad[0],
    )
    return tuple(out[None] for out in outs)


def solution(mesh):
    rows = P("rep", "fsdp", None)
    return jax.shard_map(
        per_device,
        mesh=mesh,
        in_specs=(rows, P("rep", "fsdp"), P(), rows, rows, rows, rows),
        out_specs=(rows, rows, rows),
        check_vma=False,
    )
```

time: 165 us -> 163 us (0.988)
  the two profiles are of different devices: /device:TPU:316 before, /device:TPU:1 now
where the time goes in v3:
time: 163 us; the launch traced here: 162 us
  Pallas kernels  158 us (97%)
  local copies, waits for them, and re-layouts  2.34 us (1%)
    pallas_call x1, Pallas kernels, per_device(): lax.switch(step_index[0] % bit_total, [branch(bit) for bit in range(bit_t...  158 us

profile of v3, /device:TPU:1, one launch (start us, length us, event | category | flops | bytes accessed | tf_op | source)
XLA Modules:
  0.0 162.4 jit_solution(10394495917215514667)
XLA Ops:
  1.4 0.1 pad_maximum_fusion
  1.5 158.6 %conditional.1 = ((bf16[640,384]{1,0:T(8,128)(2,1)S(1)}, bf16[640,384]{1,0:T(8,128)(2,1)S(1)}, bf16[640,384]{1,0:T(8,128)(2,1)S(1)})) conditional(s32[]{:T(128)} %clamp.3, (bf16[1,192,5120]{2,1,0:T(8,128)(2,1)}, bf16[1,640,384]{2,1,0:T(8,128)(2,1)}, bf16[1,640,384]{2,1,0:T(8,128)(2,1)}, ...), branch_computations={%region_0.1_spmd, %region_1.2_spmd, %region_2.3_spmd, %region_3.4_... | conditional | bytes 8 | solution.py:447
  1.6 158.2 %branch_3_fun.1 = (bf16[640,384]{1,0:T(8,128)(2,1)S(1)}, bf16[640,384]{1,0:T(8,128)(2,1)S(1)}, bf16[640,384]{1,0:T(8,128)(2,1)S(1)}) custom-call(f32[2]{0:T(128)S(1)} %get-tuple-element.180.coef_ref, s32[1,192]{1,0:T(1,128)} %get-tuple-element.181.doc_ref, f32[192,256]{1,0:T(8,128)} %get-tuple-element.182.tab_ref, bf16[192,5120]{1,0:T(8,128)(2,1)} %bitcast.37, ...), custom_call_target="tpu_custom_call" | custom-call | tf_op jit(solution)/shard_map/cond/branch_3_fun/pallas_call | solution.py:447
  160.1 0.8 copy.33
  160.9 0.8 copy.34
  161.7 0.8 copy.35

commit v4 on v3

--- a/solution.py
+++ b/solution.py
@@ -1,4 +1,5 @@
 import functools
+import math
 
 import jax
 import jax.numpy as jnp
@@ -21,6 +22,11 @@
 NORM_ROWS = 32
 PART = 256
 CHUNK = 64
+AHEAD = 3
+LAG = 2
+MIX_LAG = 2
+LOG_ONE = math.log(BETA_ONE)
+LOG_TWO = math.log(BETA_TWO)
 
 
 def rotary_tables(length, head_dim):
@@ -67,12 +73,12 @@
 
 def kernel(
     bit, hops,
-    coef_ref, doc_ref, tab_ref, act_hbm, w_hbm, first_hbm, second_hbm, og_hbm,
-    mixed_hbm, first_out, second_out,
+    step_ref, doc_ref, tab_ref, act_hbm, w_hbm, first_hbm, second_hbm, og_hbm,
+    mixed_out, first_out, second_out,
     act_v, keep0, keep1, away0, away1, skeep0, skeep1, saway0, saway1, xt0, xt1, w_own, w0, w1,
     mask, pacc, pacc0, pacc1, rec, rec0, rec1, psend, pz, g_ref,
-    tsend, trecv, first_v, second_v, og_v, upd, prt, mix_v, first_o, second_o,
-    loc_sem, out_sem, w_send, w_recv, x_send, x_recv, p_send, p_recv, g_send, g_recv, rs_send, rs_recv, sw_send, sw_recv,
+    tsend, trecv, first_v, second_v, og_v, t_own, upd, prt,
+    loc_sem, w_send, w_recv, x_send, x_recv, p_send, p_recv, g_send, g_recv, rs_send, rs_recv, sw_send, sw_recv,
 ):
     rep = lax.axis_index("rep")
     own = lax.axis_index("fsdp")
@@ -246,17 +252,14 @@
     for n in (2, 3, 4):
         g_copies[n].wait_recv()
 
-    def part_rows(i):
-        return pl.ds(pl.multiple_of(i * CHUNK, 16), CHUNK)
-
     def rows_of(part, i):
         return pl.ds(pl.multiple_of(part * depth0 + i * CHUNK, 16), CHUNK)
 
-    def term(slot, part, i):
+    def term(slot, part):
         if part == 0:
-            return dot(xt0[slot, part_rows(i), :], g_ref[: 4 * seq, :], plain)
-        return dot(xt1[slot, part_rows(i), : 2 * seq], g_ref[: 2 * seq, :], plain) + dot(
-            xt1[slot, part_rows(i), 2 * seq :], g_ref[4 * seq :, :], plain
+            return dot(xt0[slot], g_ref[: 4 * seq, :], plain)
+        return dot(xt1[slot, :, : 2 * seq], g_ref[: 2 * seq, :], plain) + dot(
+            xt1[slot, :, 2 * seq :], g_ref[4 * seq :, :], plain
         )
 
     def rs_copy(part, i):
@@ -268,90 +271,63 @@
         rows = rows_of(part, i)
         return remote(upd.at[rows], prt.at[rows], sw_send.at[part, i], sw_recv.at[part, i], partner)
 
-    def out_copies(part, i):
-        rows = rows_of(part, i)
-        return [
-            pltpu.make_async_copy(first_o.at[rows], first_out.at[rows], out_sem.at[0, part, i]),
-            pltpu.make_async_copy(second_o.at[rows], second_out.at[rows], out_sem.at[1, part, i]),
-        ]
-
-    def mix_copy(part, i):
-        rows = rows_of(part, i)
-        return pltpu.make_async_copy(mix_v.at[rows], mixed_hbm.at[rows], out_sem.at[2, part, i])
-
-    def send_term(part, i):
-        tsend[rows_of(part, i), :] = term(1, part, i).astype(BF16)
-        rs_copy(part, i).start()
+    all_rows = (pl.ds(0, depth0), pl.ds(depth0, depth1))
+    chunks = (chunks0, chunks1)
+    for part in (0, 1):
+        tsend[all_rows[part], :] = term(1, part).astype(BF16)
+        for i in range(AHEAD):
+            rs_copy(part, i).start()
+    for part in (0, 1):
+        t_own[all_rows[part], :] = term(0, part)
+    load_first.wait()
+    load_second.wait()
+    count = jnp.full((1, cols), step_ref[0] + 1, jnp.int32).astype(F32)
+    fix_one = 1.0 - jnp.exp(count * LOG_ONE)
+    fix_two = 1.0 - jnp.exp(count * LOG_TWO)
 
     def update(part, i):
         rows = rows_of(part, i)
-        grad = term(0, part, i)
         rs_copy(part, i).wait_recv()
-        grad = grad + trecv[rows, :].astype(F32)
+        grad = t_own[rows, :] + trecv[rows, :].astype(F32)
         weights = w_own[rows, :].astype(F32)
         first_new = BETA_ONE * first_v[rows, :].astype(F32) + (1.0 - BETA_ONE) * grad
         second_new = BETA_TWO * second_v[rows, :].astype(F32) + (1.0 - BETA_TWO) * grad * grad
-        first_hat = first_new / coef_ref[0]
-        second_hat = second_new / coef_ref[1]
+        first_hat = first_new / fix_one
+        second_hat = second_new / fix_two
         updated = weights - LEARN_RATE * (first_hat / (jnp.sqrt(second_hat) + ADAM_EPS) + DECAY_RATE * weights)
         upd[rows, :] = updated.astype(BF16)
         swap_copy(part, i).start()
-        first_o[rows, :] = first_new.astype(BF16)
-        second_o[rows, :] = second_new.astype(BF16)
-        for copy in out_copies(part, i):
-            copy.start()
+        first_out[rows, :] = first_new.astype(BF16)
+        second_out[rows, :] = second_new.astype(BF16)
 
     def mix(part, i):
         rows = rows_of(part, i)
         swap_copy(part, i).wait_recv()
-        mix_v[rows, :] = ((upd[rows, :].astype(F32) + prt[rows, :].astype(F32)) * 0.5).astype(BF16)
-        mix_copy(part, i).start()
-
-    def finish(part, i):
-        rs_copy(part, i).wait_send()
-        swap_copy(part, i).wait_send()
-        for copy in out_copies(part, i):
-            copy.wait()
-        mix_copy(part, i).wait()
-
-    def over_chunks(*calls):
-        def both(i, carry):
-            for call in calls:
-                call(0, i)
-                call(1, i)
-            return carry
-
-        def rest(i, carry):
-            for call in calls:
-                call(1, i)
-            return carry
-
-        lax.fori_loop(0, chunks0, both, 0)
-        lax.fori_loop(chunks0, chunks1, rest, 0)
-
-    over_chunks(send_term)
-    load_first.wait()
-    load_second.wait()
-
-    update(0, 0)
-    update(1, 0)
-
-    def steady(i, carry):
-        update(0, i)
-        mix(0, i - 1)
-        update(1, i)
-        mix(1, i - 1)
+        mixed_out[rows, :] = ((upd[rows, :].astype(F32) + prt[rows, :].astype(F32)) * 0.5).astype(BF16)
+
+    def stage(i, carry):
+        for part in (0, 1):
+
+            @pl.when(i < chunks[part] - AHEAD)
+            def _():
+                rs_copy(part, i).wait_send()
+                rs_copy(part, i + AHEAD).start()
+
+        for part in (0, 1):
+
+            @pl.when((i >= LAG) & (i < chunks[part] + LAG))
+            def _():
+                update(part, i - LAG)
+
+        for part in (0, 1):
+
+            @pl.when((i >= LAG + MIX_LAG) & (i < chunks[part] + LAG + MIX_LAG))
+            def _():
+                mix(part, i - LAG - MIX_LAG)
+
         return carry
 
-    def steady_rest(i, carry):
-        update(1, i)
-        mix(1, i - 1)
-        return carry
-
-    lax.fori_loop(1, chunks0, steady, 0)
-    mix(0, chunks0 - 1)
-    lax.fori_loop(chunks0, chunks1, steady_rest, 0)
-    mix(1, chunks1 - 1)
+    lax.fori_loop(0, chunks1 + LAG + MIX_LAG, stage, 0)
 
     for copy in [send_w0, send_w1, give, give0, give1, back0, back1] + g_copies:
         copy.wait_send()
@@ -361,15 +337,17 @@
         for part in (0, 1):
             to_pair(part, 0, c).wait_send()
             to_pair(part, 1, c).wait_send()
-    over_chunks(finish)
+    for part in (0, 1):
+        for i in range(chunks[part] - AHEAD, chunks[part]):
+            rs_copy(part, i).wait_send()
+        for i in range(chunks[part]):
+            swap_copy(part, i).wait_send()
 
 
 def per_device(activations, doc_ids, step_index, proj_weights, first_moment, second_moment, out_grad):
     hops = lax.axis_size("fsdp") // 2
     seq, width = activations.shape[1:]
     depth, cols = proj_weights.shape[1:]
-    count = (step_index[0] + 1).astype(F32)
-    coef = jnp.stack([1.0 - jnp.power(BETA_ONE, count), 1.0 - jnp.power(BETA_TWO, count)])
     tables = jnp.asarray(rotary_tables(seq, cols // 3))
     dma, vmem = pltpu.SemaphoreType.DMA, pltpu.VMEM
     rest = depth - PART
@@ -387,7 +365,7 @@
                 pl.BlockSpec(memory_space=pltpu.VMEM),
             ]
             + [pl.BlockSpec(memory_space=pl.ANY)] * 5,
-            out_specs=(pl.BlockSpec(memory_space=pl.ANY),) * 3,
+            out_specs=(pl.BlockSpec(memory_space=pltpu.VMEM),) * 3,
             scratch_shapes=[
                 vmem((seq, width), BF16),
                 vmem((2, 4 * seq, PART), BF16),
@@ -418,13 +396,10 @@
                 row_vmem,
                 row_vmem,
                 vmem((seq, cols // 3), BF16),
-                row_vmem,
-                row_vmem,
-                row_vmem,
+                vmem((depth, cols), F32),
                 row_vmem,
                 row_vmem,
                 dma((5,)),
-                dma((3, 2, stages)),
                 dma((2,)),
                 dma((2,)),
                 dma((8, PIECES)),
@@ -445,9 +420,9 @@
 
     bit_total = lax.axis_size("rep").bit_length() - 1
     outs = lax.switch(
-        step_index[0] % bit_total,
+        lax.rem(step_index[0], bit_total),
         [branch(bit) for bit in range(bit_total)],
-        coef, doc_ids, tables, activations[0], proj_weights[0], first_moment[0], second_moment[0], out_grad[0],
+        step_index, doc_ids, tables, activations[0], proj_weights[0], first_moment[0], second_moment[0], out_grad[0],
     )
     return tuple(out[None] for out in outs)
 

time: 163 us -> 150 us (0.920)
  Pallas kernels: 158 us -> 144 us
    pallas_call x1, Pallas kernels: 158 us -> 144 us  [per_device(): lax.switch(lax.rem(step_index[0], bit_total), [branch(bit) for bit in ran...]
where the time goes in v4:
time: 150 us; the launch traced here: 149 us
  Pallas kernels  144 us (96%)
  local copies, waits for them, and re-layouts  2.34 us (2%)
    pallas_call x1, Pallas kernels, per_device(): lax.switch(lax.rem(step_index[0], bit_total), [branch(bit) for bit in ran...  144 us

profile of v4, /device:TPU:1, one launch (start us, length us, event | category | flops | bytes accessed | tf_op | source)
XLA Modules:
  0.0 148.9 jit_solution(8995250104958031526)
XLA Ops:
  1.3 145.3 %conditional.1 = ((bf16[640,384]{1,0:T(8,128)(2,1)S(1)}, bf16[640,384]{1,0:T(8,128)(2,1)S(1)}, bf16[640,384]{1,0:T(8,128)(2,1)S(1)})) conditional(s32[]{:T(128)} %bitcast, (s32[1]{0:T(128)}, s32[1,192]{1,0:T(1,128)}, f32[192,256]{1,0:T(8,128)}, bf16[192,5120]{1,0:T(8,128)(2,1)}, bf16[640,384]{1,0:T(8,128)(2,1)}, ...), branch_computations={%region_0.0_spmd, %region_1.0_spmd, %region_2.0_spmd, %region_3.0_... | conditional | bytes 8 | solution.py:422
  1.8 144.5 %branch_5_fun.1 = (bf16[640,384]{1,0:T(8,128)(2,1)S(1)}, bf16[640,384]{1,0:T(8,128)(2,1)S(1)}, bf16[640,384]{1,0:T(8,128)(2,1)S(1)}) custom-call(s32[1]{0:T(128)} %get-tuple-element.172.step_ref, s32[1,192]{1,0:T(1,128)} %get-tuple-element.173.doc_ref, f32[192,256]{1,0:T(8,128)} %get-tuple-element.174.tab_ref, bf16[192,5120]{1,0:T(8,128)(2,1)} %get-tuple-element.175.act_hbm, ...), custom_call_target="tpu_custom_call" | custom-call | tf_op jit(solution)/shard_map/cond/branch_5_fun/pallas_call | solution.py:422
  146.6 0.8 copy.33
  147.4 0.8 copy.34
  148.2 0.8 copy.35

commit v5 on v2

v5 whole, which is shorter than its diff:
```python
import functools
import math

import jax
import jax.numpy as jnp
import numpy as np
from jax import lax
from jax.experimental import pallas as pl
from jax.experimental.pallas import tpu as pltpu
from jax.sharding import PartitionSpec as P

BETA_ONE = 0.9
BETA_TWO = 0.95
LEARN_RATE = 0.002
DECAY_RATE = 0.1
ADAM_EPS = 1e-08

MESH = pl.DeviceIdType.MESH
F32 = jnp.float32
BF16 = jnp.bfloat16
PIECES = 2
NORM_ROWS = 32
CHUNK = 64
AHEAD = 3
LAG = 2
MIX_LAG = 2
LOG_ONE = math.log(BETA_ONE)
LOG_TWO = math.log(BETA_TWO)


def rotary_tables(length, head_dim):
    position = np.arange(length, dtype=np.float32)
    inverse = np.float32(10000.0) ** (-(np.arange(head_dim // 2, dtype=np.float32) * np.float32(2.0 / head_dim)))
    angles = (position[:, None] * inverse[None, :]).astype(np.float32)
    cosine, sine = np.cos(angles), np.sin(angles)
    return np.concatenate([cosine, cosine, -sine, sine], axis=1).astype(np.float32)


def dot(a, b, contract, precision=None):
    return lax.dot_general(a, b, ((contract[0], contract[1]), ((), ())), precision=precision, preferred_element_type=F32)


def attention_grad(projected, allowed, tables, out_grad):
    length, width = projected.shape
    hd = width // 3
    high = lax.Precision.HIGHEST
    cosine, sine = tables[:, :hd], tables[:, hd:]

    def rotate(x):
        return x * cosine + pltpu.roll(x, hd // 2, 1) * sine

    def rotate_back(x):
        return x * cosine - pltpu.roll(x, hd // 2, 1) * sine

    query = rotate(projected[:, :hd].astype(F32))
    keys = rotate(projected[:, hd : 2 * hd].astype(F32))
    values = projected[:, 2 * hd :]
    scale = hd ** (-0.5)
    scores = dot(query, keys, ((1,), (1,)), high) * scale
    scores = jnp.where(allowed, scores, -1e30)
    expo = jnp.exp(scores - jnp.max(scores, axis=1, keepdims=True))
    probs = expo / jnp.sum(expo, axis=1, keepdims=True)
    probs_low = probs.astype(BF16)
    grad_values = dot(probs_low, out_grad, ((0,), (0,)))
    grad_probs = dot(out_grad, values, ((1,), (1,)))
    inner = jnp.sum(grad_probs * probs, axis=1, keepdims=True)
    grad_scores = probs * (grad_probs - inner) * scale
    grad_query = rotate_back(dot(grad_scores, keys, ((1,), (0,)), high))
    grad_keys = rotate_back(dot(grad_scores, query, ((0,), (0,)), high))
    return grad_query.astype(BF16), grad_keys.astype(BF16), grad_values.astype(BF16)


def kernel(
    bit, hops,
    step_ref, doc_ref, tab_ref, act_hbm, w_hbm, first_hbm, second_hbm, og_hbm,
    out_ref,
    act_v, keep, to_pair, to_cross, to_sib, xt, wall, mask, pacc, rec, psend, pz, g_ref,
    tsend, trecv, first_v, second_v, og_v, t_own, upd, prt,
    loc_sem, w_sem, x_send, x_recv, p_send, p_recv, g_send, g_recv, rs_send, rs_recv, sw_send, sw_recv,
):
    rep = lax.axis_index("rep")
    own = lax.axis_index("fsdp")
    z, core = own // 2, own % 2
    step = 1 - 2 * ((z + core) % 2)
    z_pair, z_next, z_far = (z + step + hops) % hops, (z - step + hops) % hops, (z + 2) % hops
    pair = (rep, z_pair * 2 + core)
    pair_cross = (rep, z_pair * 2 + 1 - core)
    following = (rep, z_next * 2 + core)
    next_cross = (rep, z_next * 2 + 1 - core)
    sibling = (rep, z * 2 + (1 - core))
    distance = 2**bit
    partner = (rep + (1 - 2 * ((rep // distance) % 2)) * distance, own)
    seq, width = act_v.shape
    depth, cols = wall.shape[1:]
    hd = cols // 3
    chunks = depth // CHUNK

    def remote(src, dst, send, recv, device):
        return pltpu.make_async_remote_copy(
            src_ref=src, dst_ref=dst, send_sem=send, recv_sem=recv, device_id=device, device_id_type=MESH
        )

    load_act = pltpu.make_async_copy(act_hbm, act_v, loc_sem.at[0])
    load_w = pltpu.make_async_copy(w_hbm, wall.at[0], loc_sem.at[1])
    load_first = pltpu.make_async_copy(first_hbm, first_v, loc_sem.at[2])
    load_second = pltpu.make_async_copy(second_hbm, second_v, loc_sem.at[3])
    load_og = pltpu.make_async_copy(og_hbm, og_v, loc_sem.at[4])
    for load in (load_act, load_w, load_first, load_second, load_og):
        load.start()

    barrier = pltpu.get_barrier_semaphore()
    greeted = (pair, pair_cross, following, next_cross, sibling, partner)
    for device in greeted:
        pl.semaphore_signal(barrier, inc=1, device_id=device, device_id_type=MESH)
    pl.semaphore_wait(barrier, len(greeted))

    send_w = remote(w_hbm, wall.at[1], w_sem.at[0], w_sem.at[1], following)
    send_w.start()

    load_act.wait()
    piece = seq // PIECES

    def rows_at(base, c):
        return pl.ds(pl.multiple_of(base + c * piece, 16), piece)

    def trade(n, c):
        src, base, device = ((to_pair, 2 * seq, pair), (to_cross, 3 * seq, next_cross), (to_sib, seq, sibling))[n]
        return remote(src.at[:, rows_at(0, c)], keep.at[:, rows_at(base, c)], x_send.at[n, c], x_recv.at[n, c], device)

    places = (
        (z_pair, core, to_pair, 0), (z_far, core, to_pair, 1),
        (z_next, 1 - core, to_cross, 0), (z_far, 1 - core, to_cross, 1),
        (z, 1 - core, to_sib, 0), (z_pair, 1 - core, to_sib, 1),
        (z, core, keep, 0), (z_next, core, keep, 1),
    )

    def norm_piece(c, carry):
        def norm_rows(i, inner):
            rows = pl.ds(pl.multiple_of(c * piece + i * NORM_ROWS, 16), NORM_ROWS)
            values = act_v[rows, :].astype(F32)
            scale = lax.rsqrt(jnp.sum(values * values, axis=-1, keepdims=True) * (1.0 / width) + 1e-05)
            for chip, which, ref, slot in places:
                block = pl.ds(pl.multiple_of((chip * 2 + which) * depth, 128), depth)
                ref[slot, rows, :] = (act_v[rows, block].astype(F32) * scale).astype(BF16)
            return inner

        lax.fori_loop(0, piece // NORM_ROWS, norm_rows, 0)
        for n in range(3):
            trade(n, c).start()
        return carry

    lax.fori_loop(0, PIECES, norm_piece, 0)

    rows = lax.broadcasted_iota(jnp.int32, (seq, seq), 0)
    columns = lax.broadcasted_iota(jnp.int32, (seq, seq), 1)
    doc_wide = jnp.broadcast_to(doc_ref[...].astype(F32), (seq, seq))
    doc_col = jnp.sum(jnp.where(rows == columns, doc_wide, 0.0), axis=1, keepdims=True)
    mask[...] = jnp.where((columns <= rows) & (doc_wide == doc_col), 1.0, 0.0)

    for c in range(PIECES):
        trade(2, c).wait_recv()

    def turn(base):
        for slot in (0, 1):
            xt[slot, :, base : base + 2 * seq] = keep[slot, base : base + 2 * seq, :].T

    turn(0)
    load_w.wait()
    send_w.wait_recv()
    plain = ((1,), (0,))

    def project(base, count):
        part = pl.ds(base, count)
        return dot(keep[0, part, :], wall[0], plain) + dot(keep[1, part, :], wall[1], plain)

    pacc[...] = project(0, 2 * seq)
    give = remote(pacc.at[pl.ds(seq, seq)], rec, p_send.at[0], p_recv.at[0], sibling)
    give.start()
    backs = [
        remote(psend.at[n], pz.at[n], p_send.at[1 + n], p_recv.at[1 + n], device)
        for n, device in enumerate((pair, pair_cross))
    ]
    for n in (0, 1):
        for c in range(PIECES):
            trade(n, c).wait_recv()
        psend[n] = project((2 + n) * seq, seq).astype(BF16)
        backs[n].start()
    turn(2 * seq)
    load_og.wait()
    give.wait_recv()
    for copy in backs:
        copy.wait_recv()
    projected = (pacc[:seq, :] + rec[...] + pz[0].astype(F32) + pz[1].astype(F32)).astype(BF16)
    grads = attention_grad(projected, mask[...] > 0.5, tab_ref[...], og_v[...])
    for n, grad_part in enumerate(grads):
        g_ref[:seq, n * hd : (n + 1) * hd] = grad_part

    g_copies = [
        remote(g_ref.at[pl.ds(0, seq)], g_ref.at[pl.ds(base * seq, seq)], g_send.at[n], g_recv.at[n], device)
        for n, (base, device) in enumerate(((2, pair), (3, next_cross), (1, sibling)))
    ]
    for copy in g_copies:
        copy.start()
    for copy in g_copies:
        copy.wait_recv()

    def rows_of(i):
        return pl.ds(pl.multiple_of(i * CHUNK, 16), CHUNK)

    def rs_copy(i):
        return remote(tsend.at[rows_of(i)], trecv.at[rows_of(i)], rs_send.at[i], rs_recv.at[i], following)

    def swap_copy(i):
        return remote(upd.at[rows_of(i)], prt.at[rows_of(i)], sw_send.at[i], sw_recv.at[i], partner)

    half = depth // 2
    for n in (0, 1):
        part = pl.ds(n * half, half)
        tsend[part, :] = dot(xt[1, part, :], g_ref[...], plain).astype(BF16)
        if n == 0:
            for i in range(AHEAD):
                rs_copy(i).start()
    t_own[...] = dot(xt[0], g_ref[...], plain)
    load_first.wait()
    load_second.wait()
    count = jnp.full((1, cols), step_ref[0] + 1, jnp.int32).astype(F32)
    fix_one = 1.0 - jnp.exp(count * LOG_ONE)
    fix_two = 1.0 - jnp.exp(count * LOG_TWO)

    def update(i):
        rows = rows_of(i)
        rs_copy(i).wait_recv()
        grad = t_own[rows, :] + trecv[rows, :].astype(F32)
        weights = wall[0, rows, :].astype(F32)
        first_new = BETA_ONE * first_v[rows, :].astype(F32) + (1.0 - BETA_ONE) * grad
        second_new = BETA_TWO * second_v[rows, :].astype(F32) + (1.0 - BETA_TWO) * grad * grad
        first_hat = first_new / fix_one
        second_hat = second_new / fix_two
        updated = weights - LEARN_RATE * (first_hat / (jnp.sqrt(second_hat) + ADAM_EPS) + DECAY_RATE * weights)
        upd[rows, :] = updated.astype(BF16)
        swap_copy(i).start()
        out_ref[1, rows, :] = first_new.astype(BF16)
        out_ref[2, rows, :] = second_new.astype(BF16)

    def mix(i):
        rows = rows_of(i)
        swap_copy(i).wait_recv()
        out_ref[0, rows, :] = ((upd[rows, :].astype(F32) + prt[rows, :].astype(F32)) * 0.5).astype(BF16)

    def stage(i, carry):
        @pl.when(i < chunks - AHEAD)
        def _():
            rs_copy(i).wait_send()
            rs_copy(i + AHEAD).start()

        @pl.when((i >= LAG) & (i < chunks + LAG))
        def _():
            update(i - LAG)

        @pl.when(i >= LAG + MIX_LAG)
        def _():
            mix(i - LAG - MIX_LAG)

        return carry

    lax.fori_loop(0, chunks + LAG + MIX_LAG, stage, 0)

    for copy in [send_w, give] + backs + g_copies:
        copy.wait_send()
    for c in range(PIECES):
        for n in range(3):
            trade(n, c).wait_send()
    for i in range(chunks - AHEAD, chunks):
        rs_copy(i).wait_send()
    for i in range(chunks):
        swap_copy(i).wait_send()


def per_device(activations, doc_ids, step_index, proj_weights, first_moment, second_moment, out_grad):
    hops = lax.axis_size("fsdp") // 2
    seq, width = activations.shape[1:]
    depth, cols = proj_weights.shape[1:]
    tables = jnp.asarray(rotary_tables(seq, cols // 3))
    dma, vmem = pltpu.SemaphoreType.DMA, pltpu.VMEM
    stages = depth // CHUNK
    row_vmem = vmem((depth, cols), BF16)

    def branch(bit):
        return pl.pallas_call(
            functools.partial(kernel, bit, hops),
            out_shape=jax.ShapeDtypeStruct((3, depth, cols), BF16),
            in_specs=[
                pl.BlockSpec(memory_space=pltpu.SMEM),
                pl.BlockSpec(memory_space=pltpu.VMEM),
                pl.BlockSpec(memory_space=pltpu.VMEM),
            ]
            + [pl.BlockSpec(memory_space=pl.ANY)] * 5,
            out_specs=pl.BlockSpec(memory_space=pltpu.VMEM),
            scratch_shapes=[
                vmem((seq, width), BF16),
                vmem((2, 4 * seq, depth), BF16),
                vmem((2, seq, depth), BF16),
                vmem((2, seq, depth), BF16),
                vmem((2, seq, depth), BF16),
                vmem((2, depth, 4 * seq), BF16),
                vmem((2, depth, cols), BF16),
                vmem((seq, seq), F32),
                vmem((2 * seq, cols), F32),
                vmem((seq, cols), F32),
                vmem((2, seq, cols), BF16),
                vmem((2, seq, cols), BF16),
                vmem((4 * seq, cols), BF16),
                row_vmem,
                row_vmem,
                row_vmem,
                row_vmem,
                vmem((seq, cols // 3), BF16),
                vmem((depth, cols), F32),
                row_vmem,
                row_vmem,
                dma((5,)),
                dma((2,)),
                dma((3, PIECES)),
                dma((3, PIECES)),
                dma((3,)),
                dma((3,)),
                dma((3,)),
                dma((3,)),
                dma((stages,)),
                dma((stages,)),
                dma((stages,)),
                dma((stages,)),
            ],
            compiler_params=pltpu.CompilerParams(
                collective_id=bit, has_side_effects=True, vmem_limit_bytes=40 * 2**20
            ),
        )

    bit_total = lax.axis_size("rep").bit_length() - 1
    outs = lax.switch(
        lax.rem(step_index[0], bit_total),
        [branch(bit) for bit in range(bit_total)],
        step_index, doc_ids, tables, activations[0], proj_weights[0], first_moment[0], second_moment[0], out_grad[0],
    )
    return tuple(outs[n : n + 1] for n in range(3))


def solution(mesh):
    rows = P("rep", "fsdp", None)
    return jax.shard_map(
        per_device,
        mesh=mesh,
        in_specs=(rows, P("rep", "fsdp"), P(), rows, rows, rows, rows),
        out_specs=(rows, rows, rows),
        check_vma=False,
    )
```

time: 165 us -> 146 us (0.88)
  the two profiles are of different devices: /device:TPU:316 before, /device:TPU:100 now
where the time goes in v5:
time: 146 us
  Pallas kernels  143 us (98%)
    pallas_call x1, Pallas kernels, per_device(): lax.switch(lax.rem(step_index[0], bit_total), [branch(bit) for bit in ran...  143 us

profile of v5, /device:TPU:100, one launch (start us, length us, event | category | flops | bytes accessed | tf_op | source)
XLA Modules:
  0.0 146.1 jit_solution(1981586800984946041)
XLA Ops:
  1.3 143.7 %conditional.1 = (bf16[3,640,384]{2,1,0:T(8,128)(2,1)S(1)}) conditional(s32[]{:T(128)} %bitcast, (s32[1]{0:T(128)}, s32[1,192]{1,0:T(1,128)}, f32[192,256]{1,0:T(8,128)}, bf16[192,5120]{1,0:T(8,128)(2,1)}, bf16[640,384]{1,0:T(8,128)(2,1)}, /*index=5*/bf16[640,384]{1,0:T(8,128)(2,1)}, bf16[640,384]{1,0:T(8,128)(2,1)}, ...), branch_computations={%region_0.0_spmd, %region_1.0_spmd, %region_2.0_spmd, %region_3.0_... | conditional | bytes 8 | solution.py:340
  1.3 142.9 %branch_1_fun.1 = bf16[3,640,384]{2,1,0:T(8,128)(2,1)S(1)} custom-call(s32[1]{0:T(128)} %get-tuple-element.111.step_ref, s32[1,192]{1,0:T(1,128)} %get-tuple-element.112.doc_ref, f32[192,256]{1,0:T(8,128)} %get-tuple-element.113.tab_ref, bf16[192,5120]{1,0:T(8,128)(2,1)} %get-tuple-element.114.act_hbm, bf16[640,384]{1,0:T(8,128)(2,1)} %get-tuple-element.115.w_hbm, ...), custom_call_target="tpu_custom_call" | custom-call | tf_op jit(solution)/shard_map/cond/branch_1_fun/pallas_call | solution.py:340
  145.0 1.2 fusion

commit v6 on v5

--- a/solution.py
+++ b/solution.py
@@ -75,7 +75,7 @@
     step_ref, doc_ref, tab_ref, act_hbm, w_hbm, first_hbm, second_hbm, og_hbm,
     out_ref,
     act_v, keep, to_pair, to_cross, to_sib, xt, wall, mask, pacc, rec, psend, pz, g_ref,
-    tsend, trecv, first_v, second_v, og_v, t_own, upd, prt,
+    tsend, trecv, first_v, second_v, og_v, tacc, t_own, upd, prt,
     loc_sem, w_sem, x_send, x_recv, p_send, p_recv, g_send, g_recv, rs_send, rs_recv, sw_send, sw_recv,
 ):
     rep = lax.axis_index("rep")
@@ -201,7 +201,11 @@
     ]
     for copy in g_copies:
         copy.start()
-    for copy in g_copies:
+    g_copies[2].wait_recv()
+    near, far = slice(0, 2 * seq), slice(2 * seq, 4 * seq)
+    for slot in (0, 1):
+        tacc[slot] = dot(xt[slot, :, near], g_ref[near, :], plain)
+    for copy in g_copies[:2]:
         copy.wait_recv()
 
     def rows_of(i):
@@ -213,14 +217,13 @@
     def swap_copy(i):
         return remote(upd.at[rows_of(i)], prt.at[rows_of(i)], sw_send.at[i], sw_recv.at[i], partner)
 
-    half = depth // 2
-    for n in (0, 1):
-        part = pl.ds(n * half, half)
-        tsend[part, :] = dot(xt[1, part, :], g_ref[...], plain).astype(BF16)
-        if n == 0:
+    for start, size in ((0, AHEAD * CHUNK), (AHEAD * CHUNK, depth - AHEAD * CHUNK)):
+        part = pl.ds(start, size)
+        tsend[part, :] = (tacc[1, part, :] + dot(xt[1, part, far], g_ref[far, :], plain)).astype(BF16)
+        if start == 0:
             for i in range(AHEAD):
                 rs_copy(i).start()
-    t_own[...] = dot(xt[0], g_ref[...], plain)
+    t_own[...] = tacc[0] + dot(xt[0, :, far], g_ref[far, :], plain)
     load_first.wait()
     load_second.wait()
     count = jnp.full((1, cols), step_ref[0] + 1, jnp.int32).astype(F32)
@@ -315,6 +318,7 @@
                 row_vmem,
                 row_vmem,
                 vmem((seq, cols // 3), BF16),
+                vmem((2, depth, cols), F32),
                 vmem((depth, cols), F32),
                 row_vmem,
                 row_vmem,

time: 146 us -> 154 us (1.055)
  the two profiles are of different devices: /device:TPU:100 before, /device:TPU:1 now
where the time goes in v6:
time: 154 us; the launch traced here: 157 us
  Pallas kernels  154 us (100%)
    pallas_call x1, Pallas kernels, per_device(): lax.switch(lax.rem(step_index[0], bit_total), [branch(bit) for bit in ran...  154 us

profile of v6, /device:TPU:1, one launch (start us, length us, event | category | flops | bytes accessed | tf_op | source)
XLA Modules:
  0.0 156.6 jit_solution(15725033228527583719)
XLA Ops:
  1.3 154.2 %conditional.1 = (bf16[3,640,384]{2,1,0:T(8,128)(2,1)S(1)}) conditional(s32[]{:T(128)} %bitcast, (s32[1]{0:T(128)}, s32[1,192]{1,0:T(1,128)}, f32[192,256]{1,0:T(8,128)}, bf16[192,5120]{1,0:T(8,128)(2,1)}, bf16[640,384]{1,0:T(8,128)(2,1)}, /*index=5*/bf16[640,384]{1,0:T(8,128)(2,1)}, bf16[640,384]{1,0:T(8,128)(2,1)}, ...), branch_computations={%region_0.0_spmd, %region_1.0_spmd, %region_2.0_spmd, %region_3.0_... | conditional | bytes 8 | solution.py:344
  1.5 153.6 %branch_3_fun.1 = bf16[3,640,384]{2,1,0:T(8,128)(2,1)S(1)} custom-call(s32[1]{0:T(128)} %get-tuple-element.127.step_ref, s32[1,192]{1,0:T(1,128)} %get-tuple-element.128.doc_ref, f32[192,256]{1,0:T(8,128)} %get-tuple-element.129.tab_ref, bf16[192,5120]{1,0:T(8,128)(2,1)} %get-tuple-element.130.act_hbm, bf16[640,384]{1,0:T(8,128)(2,1)} %get-tuple-element.131.w_hbm, ...), custom_call_target="tpu_custom_call" | custom-call | tf_op jit(solution)/shard_map/cond/branch_3_fun/pallas_call | solution.py:344
  155.4 1.2 fusion
